TPU v7x, 128 devices: a whole 4x4x4 slice. The times are simulated.
128 devices in a mesh: dp: 8 (over x_hi, z), tensor: 16 (over x_lo, y, core).
Axes of the slice: x: 4 (x_hi: 2, x_lo: 2; x = x_hi * 2 + x_lo), y: 4, z: 4, core: 2. Of those that a mesh axis runs over, the one named last changes fastest.
Arguments:
- history: bfloat16 [17, 16384, 2048], P(None, ('dp', 'tensor')), may hold values from -6 to 6
- cotangent: bfloat16 [16384, 2048], P(('dp', 'tensor')), may hold values from -6 to 6
- lengths: int32 [8, 4], replicated, may hold values from 0 to 2048, as said below
- mix_gain: float32 [2048], replicated, may hold values from 0.5 to 1.5
- mix_first: float32 [2048, 68], replicated, may hold values from -0.125 to 0.125
- mix_second: float32 [68, 68], replicated, may hold values from -0.3 to 0.3
- mix_bias: float32 [68], replicated, may hold values from -1.8 to 1.8
- gain_query: float32 [2048], replicated, may hold values from 0.5 to 1.5
- gain_key: float32 [2048], replicated, may hold values from 0.5 to 1.5
- gain_value: float32 [2048], replicated, may hold values from 0.5 to 1.5
- gain_mlp: float32 [2048], replicated, may hold values from 0.5 to 1.5
- w_query: bfloat16 [2048, 2048], P(None, 'tensor'), may hold values from -0.125 to 0.125
- w_key: bfloat16 [2048, 2048], P(None, 'tensor'), may hold values from -0.125 to 0.125
- w_value: bfloat16 [2048, 2048], P(None, 'tensor'), may hold values from -0.125 to 0.125
- w_output: bfloat16 [2048, 2048], P('tensor'), may hold values from -1 to 1
- w_expand: bfloat16 [2048, 8192], P(None, 'tensor'), may hold values from -0.125 to 0.125
- w_reduce: bfloat16 [8192, 2048], P('tensor'), may hold values from -0.0625 to 0.0625
Outputs:
- output: bfloat16 [16384, 2048], P(('dp', 'tensor'))
- grad_history: bfloat16 [17, 16384, 2048], P(None, ('dp', 'tensor'))
- grad_mix_gain: float32 [2048], replicated
- grad_mix_first: float32 [2048, 68], replicated
- grad_mix_second: float32 [68, 68], replicated
- grad_mix_bias: float32 [68], replicated
- grad_gain_query: float32 [2048], replicated
- grad_gain_key: float32 [2048], replicated
- grad_gain_value: float32 [2048], replicated
- grad_gain_mlp: float32 [2048], replicated
- grad_w_query: float32 [2048, 2048], P('dp', 'tensor')
- grad_w_key: float32 [2048, 2048], P('dp', 'tensor')
- grad_w_value: float32 [2048, 2048], P('dp', 'tensor')
- grad_w_output: float32 [2048, 2048], P('tensor', 'dp')
- grad_w_expand: float32 [2048, 8192], P('dp', 'tensor')
- grad_w_reduce: float32 [8192, 2048], P('tensor', 'dp')
Inputs may be any that keep to these rules, and one draw needn't show every extreme that they name: Row g holds, in order, the lengths of the sequences packed into the 2048 tokens of data index g (0 marks an empty slot); each row sums to 2048, its longest entry is 1024 or more, and in some row one sequence fills all 2048 tokens.
All inputs are finite; a program needn't handle non-finite values.
Results may differ from a plain program's by a relative error of at most 0.019.
Values may be sent and summed in bfloat16 or wider, within the bound.
A program may use at most 320 MiB of HBM per device.

v0:
```python
import jax
import jax.numpy as jnp
from jax import lax
from jax.sharding import PartitionSpec as P

HEAD_DIM = 128
HISTORY = 17
STREAMS = 4
NORM_EPS = 1e-06
MASKED = -1e30
PRECISE = lax.Precision.HIGHEST


def swapped(x, axis, bit):
    return lax.ppermute(x, axis, [(i, i ^ 1 << bit) for i in range(lax.axis_size(axis))])


def rms_scale(values, gain_vector):
    inverse = lax.rsqrt(jnp.mean(values * values, axis=-1, keepdims=True) + NORM_EPS)
    return values * inverse * gain_vector


def matmul(left_side, right_side):
    return jnp.dot(left_side, right_side, precision=PRECISE)


def front_part(
    history_float, mix_gain, mix_first, mix_second, mix_bias, gain_query, gain_key, gain_value
):
    latest = rms_scale(history_float[HISTORY - 1], mix_gain)
    hidden = jax.nn.gelu(matmul(latest, mix_first), approximate=False)
    mixing = (matmul(hidden, mix_second) + mix_bias).reshape(
        history_float.shape[1], STREAMS, HISTORY
    )
    streams = jnp.einsum("tkj,jtd->ktd", mixing, history_float, precision=PRECISE)
    return (
        rms_scale(streams[0], gain_query),
        rms_scale(streams[1], gain_key),
        rms_scale(streams[2], gain_value),
        streams[3],
    )


def gelu_exact(values):
    return jax.nn.gelu(values, approximate=False)


def across_rows(left_side, right_side):
    return lax.dot_general(
        left_side, right_side, (((0,), (0,)), ((), ())), preferred_element_type=jnp.float32
    )


def across_cols(left_side, right_side):
    return lax.dot_general(
        left_side, right_side, (((1,), (1,)), ((), ())), preferred_element_type=jnp.float32
    )


def segment_of(places, doc_ends):
    return jnp.sum((places[:, None] >= doc_ends[None, :]).astype(jnp.int32), axis=1)


def gather_bits(piece, bit_list, join_dim, device_index):
    for bit_number in bit_list:
        partner = swapped(piece, "tensor", bit_number)
        upper = device_index // (1 << bit_number) % 2 == 1
        piece = jnp.where(
            upper,
            jnp.concatenate([partner, piece], axis=join_dim),
            jnp.concatenate([piece, partner], axis=join_dim),
        )
    return piece


def sum_bits(partial_value, bit_list, device_index, split_dim):
    for bit_number in reversed(bit_list):
        half_size = partial_value.shape[split_dim] // 2
        lower_half = lax.slice_in_dim(partial_value, 0, half_size, axis=split_dim)
        upper_half = lax.slice_in_dim(partial_value, half_size, 2 * half_size, axis=split_dim)
        upper = device_index // (1 << bit_number) % 2 == 1
        keep_half = jnp.where(upper, upper_half, lower_half)
        send_half = jnp.where(upper, lower_half, upper_half)
        partial_value = keep_half + swapped(
            send_half.astype(jnp.bfloat16), "tensor", bit_number
        ).astype(send_half.dtype)
    return partial_value


def make_scores(query_heads, key_heads, query_places, key_places, doc_ends):
    block_rows = min(512, query_heads.shape[0])
    scale_factor = HEAD_DIM ** (-0.5)
    query_segments = segment_of(query_places, doc_ends)
    key_segments = segment_of(key_places, doc_ends)

    def block_scores(block_index):
        scores = (
            jnp.einsum("qhd,khd->hqk", query_heads, key_heads, preferred_element_type=jnp.float32)
            * scale_factor
        )
        allowed = (query_places[:, None] >= key_places[None, :]) & (
            query_segments[:, None] == key_segments[None, :]
        )
        return (jnp.where(allowed[None], scores, MASKED), query_heads)

    return (block_scores, block_rows)


def on_device(
    history,
    cotangent,
    lengths,
    mix_gain,
    mix_first,
    mix_second,
    mix_bias,
    gain_query,
    gain_key,
    gain_value,
    gain_mlp,
    w_query,
    w_key,
    w_value,
    w_output,
    w_expand,
    w_reduce,
):
    shard_rows = history.shape[1]
    tensor_size = lax.axis_size("tensor")
    tok_group = shard_rows * tensor_size
    model_width = w_query.shape[0]
    tensor_index = lax.axis_index("tensor")
    low_bits = [0, 1]
    high_bits = list(range(2, tensor_size.bit_length() - 1))
    scale_factor = HEAD_DIM ** (-0.5)
    history_float = history.astype(jnp.float32)
    front_values, front_back = jax.vjp(
        front_part,
        history_float,
        mix_gain,
        mix_first,
        mix_second,
        mix_bias,
        gain_query,
        gain_key,
        gain_value,
    )
    query_norm, key_norm, value_norm, residual = front_values
    query_low = query_norm.astype(jnp.bfloat16)
    key_low = key_norm.astype(jnp.bfloat16)
    value_low = value_norm.astype(jnp.bfloat16)
    length_row = lax.dynamic_index_in_dim(lengths, lax.axis_index("dp"), 0, keepdims=False)
    doc_ends = jnp.cumsum(length_row)
    query_rows = gather_bits(query_low, high_bits, 0, tensor_index)
    key_rows = gather_bits(key_low, high_bits, 0, tensor_index)
    value_rows = gather_bits(value_low, high_bits, 0, tensor_index)
    cot_rows = gather_bits(cotangent, high_bits, 0, tensor_index)
    query_whole = gather_bits(w_query, low_bits, 1, tensor_index)
    key_whole = gather_bits(w_key, low_bits, 1, tensor_index)
    value_whole = gather_bits(w_value, low_bits, 1, tensor_index)
    output_whole = gather_bits(w_output, low_bits, 0, tensor_index)
    expand_whole = gather_bits(w_expand, low_bits, 1, tensor_index)
    reduce_whole = gather_bits(w_reduce, low_bits, 0, tensor_index)
    group_count = tensor_size // 4
    part_index = tensor_index % 4
    inner_rows = jnp.arange(shard_rows, dtype=jnp.int32)
    group_offsets = 4 * jnp.arange(group_count, dtype=jnp.int32)
    query_places = (
        (part_index + group_offsets)[:, None] * shard_rows + inner_rows[None, :]
    ).reshape(-1)
    key_places = (
        (jnp.arange(4, dtype=jnp.int32)[:, None, None] + group_offsets[None, :, None]) * shard_rows
        + inner_rows[None, None, :]
    ).reshape(-1)
    row_count = query_rows.shape[0]
    heads_here = query_whole.shape[1] // HEAD_DIM
    query_heads = (
        jnp.dot(query_rows, query_whole, preferred_element_type=jnp.float32)
        .astype(jnp.bfloat16)
        .reshape(row_count, heads_here, HEAD_DIM)
    )
    key_part = jnp.dot(key_rows, key_whole, preferred_element_type=jnp.float32).astype(jnp.bfloat16)
    value_part = jnp.dot(value_rows, value_whole, preferred_element_type=jnp.float32).astype(
        jnp.bfloat16
    )
    key_flat = gather_bits(key_part, low_bits, 0, tensor_index)
    value_flat = gather_bits(value_part, low_bits, 0, tensor_index)
    key_heads = key_flat.reshape(tok_group, heads_here, HEAD_DIM)
    value_heads = value_flat.reshape(tok_group, heads_here, HEAD_DIM)
    block_scores, block_rows = make_scores(
        query_heads, key_heads, query_places, key_places, doc_ends
    )
    block_count = row_count // block_rows

    def forward_block(block_index):
        masked, query_block = block_scores(block_index)
        top_score = jnp.max(masked, axis=-1, keepdims=True)
        exponent = jnp.exp(masked - top_score)
        row_total = jnp.sum(exponent, axis=-1, keepdims=True)
        weights_low = (exponent / row_total).astype(jnp.bfloat16)
        context_block = jnp.einsum(
            "hqk,khd->qhd", weights_low, value_heads, preferred_element_type=jnp.float32
        )
        return (context_block, top_score + jnp.log(row_total))

    context_blocks, log_totals = lax.map(forward_block, jnp.arange(block_count))
    context = context_blocks.reshape(row_count, heads_here * HEAD_DIM).astype(jnp.bfloat16)
    attended = sum_bits(
        jnp.dot(context, output_whole, preferred_element_type=jnp.float32),
        high_bits,
        tensor_index,
        0,
    )
    middle = residual + attended
    mlp_norm, norm_back = jax.vjp(rms_scale, middle, gain_mlp)
    mlp_low = mlp_norm.astype(jnp.bfloat16)
    mlp_gathered = gather_bits(mlp_low, high_bits, 0, tensor_index)
    expanded = jnp.dot(mlp_gathered, expand_whole, preferred_element_type=jnp.float32)
    activated, gelu_back = jax.vjp(gelu_exact, expanded)
    active_low = activated.astype(jnp.bfloat16)
    reduced = sum_bits(
        jnp.dot(active_low, reduce_whole, preferred_element_type=jnp.float32),
        high_bits,
        tensor_index,
        0,
    )
    output = (middle + reduced).astype(jnp.bfloat16)
    grad_w_reduce = across_rows(active_low, cot_rows)
    grad_active = across_cols(cot_rows, reduce_whole)
    (grad_expanded,) = gelu_back(grad_active)
    expand_low = grad_expanded.astype(jnp.bfloat16)
    grad_w_expand = across_rows(mlp_gathered, expand_low)
    grad_mlp_norm = sum_bits(across_cols(expand_low, expand_whole), high_bits, tensor_index, 0)
    grad_w_expand = sum_bits(grad_w_expand, low_bits, tensor_index, 1)
    grad_w_reduce = sum_bits(grad_w_reduce, low_bits, tensor_index, 0)
    grad_middle_norm, grad_gain_mlp = norm_back(grad_mlp_norm)
    grad_middle = cotangent.astype(jnp.float32) + grad_middle_norm
    middle_low = grad_middle.astype(jnp.bfloat16)
    middle_rows = gather_bits(middle_low, high_bits, 0, tensor_index)
    grad_w_output = across_rows(context, middle_rows)
    grad_context = (
        across_cols(middle_rows, output_whole)
        .astype(jnp.bfloat16)
        .reshape(row_count, heads_here, HEAD_DIM)
    )

    def backward_block(totals, block_index):
        grad_key_sum, grad_value_sum = totals
        masked, query_block = block_scores(block_index)
        weights_float = jnp.exp(masked - log_totals[block_index])
        weights_low = weights_float.astype(jnp.bfloat16)
        grad_weights = jnp.einsum(
            "qhd,khd->hqk", grad_context, value_heads, preferred_element_type=jnp.float32
        )
        row_delta = jnp.sum(grad_weights * weights_float, axis=-1, keepdims=True)
        grad_scores = (weights_float * (grad_weights - row_delta)).astype(jnp.bfloat16)
        grad_query_block = (
            jnp.einsum("hqk,khd->qhd", grad_scores, key_heads, preferred_element_type=jnp.float32)
            * scale_factor
        )
        grad_key_sum = (
            grad_key_sum
            + jnp.einsum(
                "hqk,qhd->khd", grad_scores, query_block, preferred_element_type=jnp.float32
            )
            * scale_factor
        )
        grad_value_sum = grad_value_sum + jnp.einsum(
            "hqk,qhd->khd", weights_low, grad_context, preferred_element_type=jnp.float32
        )
        return ((grad_key_sum, grad_value_sum), grad_query_block)

    zero_heads = jnp.zeros((tok_group, heads_here, HEAD_DIM), jnp.float32)
    (grad_key_sum, grad_value_sum), grad_query_blocks = lax.scan(
        backward_block, (zero_heads, zero_heads), jnp.arange(block_count)
    )
    grad_key_flat = grad_key_sum.reshape(tok_group, heads_here * HEAD_DIM)
    grad_value_flat = grad_value_sum.reshape(tok_group, heads_here * HEAD_DIM)
    grad_key_flat = sum_bits(grad_key_flat, low_bits, tensor_index, 0)
    grad_value_flat = sum_bits(grad_value_flat, low_bits, tensor_index, 0)
    grad_queries = grad_query_blocks.reshape(row_count, heads_here * HEAD_DIM).astype(jnp.bfloat16)
    grad_keys = grad_key_flat.astype(jnp.bfloat16)
    grad_values = grad_value_flat.astype(jnp.bfloat16)
    grad_w_query = across_rows(query_rows, grad_queries)
    grad_w_key = across_rows(key_rows, grad_keys)
    grad_w_value = across_rows(value_rows, grad_values)
    grad_w_query = sum_bits(grad_w_query, low_bits, tensor_index, 1)
    grad_w_key = sum_bits(grad_w_key, low_bits, tensor_index, 1)
    grad_w_value = sum_bits(grad_w_value, low_bits, tensor_index, 1)
    grad_w_output = sum_bits(grad_w_output, low_bits, tensor_index, 0)
    stream_partial = jnp.concatenate(
        [
            across_cols(grad_queries, query_whole),
            across_cols(grad_keys, key_whole),
            across_cols(grad_values, value_whole),
        ],
        axis=1,
    )
    grad_streams = sum_bits(stream_partial, high_bits, tensor_index, 0)
    front_grads = front_back(
        (
            grad_streams[:, :model_width],
            grad_streams[:, model_width : 2 * model_width],
            grad_streams[:, 2 * model_width :],
            grad_middle,
        )
    )
    grad_history = front_grads[0].astype(jnp.bfloat16)
    small_sums = lax.psum(
        (
            front_grads[1],
            front_grads[2],
            front_grads[3],
            front_grads[4],
            front_grads[5],
            front_grads[6],
            front_grads[7],
            grad_gain_mlp,
        ),
        ("dp", "tensor"),
    )
    sum_query, sum_key, sum_value, sum_output, sum_expand, sum_reduce = (
        lax.psum_scatter(
            grad_w_query.astype(jnp.bfloat16), "dp", scatter_dimension=0, tiled=True
        ).astype(jnp.float32),
        lax.psum_scatter(
            grad_w_key.astype(jnp.bfloat16), "dp", scatter_dimension=0, tiled=True
        ).astype(jnp.float32),
        lax.psum_scatter(
            grad_w_value.astype(jnp.bfloat16), "dp", scatter_dimension=0, tiled=True
        ).astype(jnp.float32),
        lax.psum_scatter(
            grad_w_output.astype(jnp.bfloat16), "dp", scatter_dimension=1, tiled=True
        ).astype(jnp.float32),
        lax.psum_scatter(
            grad_w_expand.astype(jnp.bfloat16), "dp", scatter_dimension=0, tiled=True
        ).astype(jnp.float32),
        lax.psum_scatter(
            grad_w_reduce.astype(jnp.bfloat16), "dp", scatter_dimension=1, tiled=True
        ).astype(jnp.float32),
    )
    return (
        output,
        grad_history,
        small_sums[0],
        small_sums[1],
        small_sums[2],
        small_sums[3],
        small_sums[4],
        small_sums[5],
        small_sums[6],
        small_sums[7],
        sum_query,
        sum_key,
        sum_value,
        sum_output,
        sum_expand,
        sum_reduce,
    )


def solution(mesh):
    placed = (
        P(None, ("dp", "tensor"), None),
        P(("dp", "tensor"), None),
        P(),
        P(),
        P(),
        P(),
        P(),
        P(),
        P(),
        P(),
        P(),
        P(None, "tensor"),
        P(None, "tensor"),
        P(None, "tensor"),
        P("tensor", None),
        P(None, "tensor"),
        P("tensor", None),
    )
    return jax.shard_map(
        on_device,
        mesh=mesh,
        in_specs=placed,
        out_specs=(
            P(("dp", "tensor"), None),
            P(None, ("dp", "tensor"), None),
            P(),
            P(),
            P(),
            P(),
            P(),
            P(),
            P(),
            P(),
            P("dp", "tensor"),
            P("dp", "tensor"),
            P("dp", "tensor"),
            P("tensor", "dp"),
            P("dp", "tensor"),
            P("tensor", "dp"),
        ),
        check_vma=False,
    )
```

profile of v0, /device:TPU:1, one launch (start us, length us, event | category | flops | bytes accessed | tf_op | source)
XLA Modules:
  0.0 1349.2 jit_solution(5649538605081657744)
XLA Ops:
  16.1 19.8 %fusion.22 = f32[4,128,2048]{2,0,1:T(4,128)S(1)} fusion(f32[128,4,17]{2,1,0:T(4,128)S(1)} %copy.62, bf16[17,128,2048]{2,1,0:T(8,128)(2,1)} %param.17), kind=kOutput, calls=%fused_computation.55 | convolution fusion | flops 213909504 | bytes 13142016 | tf_op jit(solution)/shard_map/jvp(tkj,jtd->ktd)/dot_general | solution.py:35
  51.3 16.1 %collective-permute-done.10 = bf16[128,2048]{1,0:T(8,128)(2,1)} collective-permute-done((bf16[128,2048]{1,0:T(8,128)(2,1)S(1)}, bf16[128,2048]{1,0:T(8,128)(2,1)}, u32[]{:S(2)}, u32[]{:S(2)}) %collective-permute-start.10) | collective-permute-done | bytes 524320 | tf_op jit(solution)/shard_map/ppermute | solution.py:15
  81.2 19.9 %collective-permute-done.6 = bf16[128,2048]{1,0:T(8,128)(2,1)S(1)} collective-permute-done((bf16[128,2048]{1,0:T(8,128)(2,1)S(1)}, bf16[128,2048]{1,0:T(8,128)(2,1)S(1)}, u32[]{:S(2)}, u32[]{:S(2)}) %collective-permute-start.6) | collective-permute-done | bytes 524320 | tf_op jit(solution)/shard_map/ppermute | solution.py:15
  102.9 5.0 convolution_convert_fusion.1
  110.7 13.2 collective-permute-done.3
  132.9 13.5 collective-permute-done.9
  151.4 17.4 %collective-permute-done.15 = bf16[1024,512]{0,1:T(8,128)(2,1)S(1)} collective-permute-done((bf16[1024,512]{0,1:T(8,128)(2,1)S(1)}, bf16[1024,512]{0,1:T(8,128)(2,1)S(1)}, u32[]{:S(2)}, u32[]{:S(2)}) %collective-permute-start.15) | collective-permute-done | bytes 1048608 | tf_op jit(solution)/shard_map/ppermute | solution.py:15
  168.8 8.6 fusion.112
  177.4 8.1 fusion.1
  185.5 28.3 %collective-permute-done.5 = bf16[1024,512]{0,1:T(8,128)(2,1)} collective-permute-done((bf16[1024,512]{0,1:T(8,128)(2,1)}, bf16[1024,512]{0,1:T(8,128)(2,1)}, u32[]{:S(2)}, u32[]{:S(2)}) %collective-permute-start.5) | collective-permute-done | bytes 1048608 | tf_op jit(solution)/shard_map/ppermute | solution.py:15
  213.9 8.3 fusion.30
  227.4 5.1 maximum_select_fusion.2
  233.7 16.4 %collective-permute-done.18 = bf16[256,2048]{1,0:T(8,128)(2,1)S(1)} collective-permute-done((bf16[256,2048]{1,0:T(8,128)(2,1)S(1)}, bf16[256,2048]{1,0:T(8,128)(2,1)S(1)}, u32[]{:S(2)}, u32[]{:S(2)}) %collective-permute-start.18) | collective-permute-done | bytes 1048608 | tf_op jit(solution)/shard_map/ppermute | solution.py:15
  254.3 80.8 %collective-permute-done.19 = bf16[128,2048]{1,0:T(8,128)(2,1)S(1)} collective-permute-done((bf16[128,2048]{1,0:T(8,128)(2,1)S(1)}, bf16[128,2048]{1,0:T(8,128)(2,1)S(1)}, u32[]{:S(2)}, u32[]{:S(2)}) %collective-permute-start.19) | collective-permute-done | bytes 524320 | tf_op jit(solution)/shard_map/ppermute | solution.py:15
  338.4 11.0 collective-permute-done.20
  351.9 3.7 maximum_select_fusion.3
  356.1 5.9 collective-permute-done.28
  366.0 5.8 collective-permute-done.21
  371.8 26.3 %multiply_convert_fusion.1 = (bf16[512,2048]{1,0:T(8,128)(2,1)}, f32[512,2048]{1,0:T(8,128)}, f32[512,2048]{1,0:T(8,128)}) fusion(bf16[2048,1024]{1,0:T(8,128)(2,1)} %copy-done.24, bf16[2048,1024]{1,0:T(8,128)(2,1)} %copy-done.80, pred[]{:T(512)S(6)} %eq.154, bf16[256,2048]{1,0:T(8,128)(2,1)} %copy-done.44, bf16[256,2048]{1,0:T(8,128)(2,1)} %collective-permute-done.21, ...), kind=kOutput, calls=%fused_computation.37 | convolution fusion | flops 4410310656 | bytes 20971522 | tf_op jit(solution)/shard_map/dot_general | solution.py:218
  398.1 52.9 %collective-permute-done.25 = bf16[1024,2048]{1,0:T(8,128)(2,1)} collective-permute-done((bf16[1024,2048]{1,0:T(8,128)(2,1)}, bf16[1024,2048]{1,0:T(8,128)(2,1)}, u32[]{:S(2)}, u32[]{:S(2)}) %collective-permute-start.25) | collective-permute-done | bytes 4194336 | tf_op jit(solution)/shard_map/ppermute | solution.py:15
  451.0 20.3 %add_convert_fusion.2 = bf16[512,2048]{1,0:T(8,128)(2,1)} fusion(f32[512,2048]{1,0:T(8,128)} %get-tuple-element.156, f32[512,2048]{1,0:T(8,128)} %get-tuple-element.171, bf16[1024,2048]{1,0:T(8,128)(2,1)} %maximum_select_fusion.3, bf16[1024,2048]{1,0:T(8,128)(2,1)} %collective-permute-done.25, pred[]{:T(512)S(6)} %eq.154, ...), kind=kOutput, calls=%fused_computation.36 | convolution fusion | flops 4356833280 | bytes 20971522 | tf_op jit(solution)/shard_map/dot_general | solution.py:55
  471.3 10.6 fusion.27
  482.2 10.2 fusion.26
  494.3 7.0 fusion.54
  501.3 34.4 %collective-permute-done.30 = bf16[256,2048]{1,0:T(8,128)(2,1)} collective-permute-done((bf16[256,2048]{1,0:T(8,128)(2,1)S(1)}, bf16[256,2048]{1,0:T(8,128)(2,1)}, u32[]{:S(2)}, u32[]{:S(2)}) %collective-permute-start.30) | collective-permute-done | bytes 1048608 | tf_op jit(solution)/shard_map/ppermute | solution.py:15
  543.8 4.5 collective-permute-done.31
  549.5 10.4 collective-permute-done.27
  566.5 4.8 collective-permute-done.32
  572.9 7.1 fusion.53
  580.0 5.8 copy-done.4
  589.7 4.3 convolution_convert_fusion
  595.0 3.7 fusion.19
  598.7 14.3 %multiply_reduce_fusion = (f32[4,512]{1,0:T(4,128)S(1)}, f32[4,512,2048]{2,1,0:T(8,128)}) fusion(f32[4,512,2048]{2,1,0:T(8,128)} %get-tuple-element.170, f32[4,512]{1,0:T(4,128)S(1)} %log_add_fusion, bf16[512,4,128]{0,2,1:T(8,128)(2,1)S(1)} %bitcast.140, bf16[1024,4,128]{0,2,1:T(8,128)(2,1)S(1)} %copy-done.29, bf16[1024,4,128]{0,2,1:T(8,128)(2,1)} %bitcast.5, ...), kind=kOutput, calls=%fused_computation.3 | convolution fusion | flops 1095759872 | bytes 36192256 | tf_op jit(solution)/shard_map/while/body/eval_jaxpr/qhd,khd->hqk/dot_general | solution.py:252
  613.1 15.9 %multiply_convert_fusion = bf16[4,512,2048]{2,1,0:T(8,128)(2,1)} fusion(f32[4,512,2048]{2,1,0:T(8,128)} %get-tuple-element.173, f32[4,512,2048]{2,1,0:T(8,128)} %get-tuple-element.170, f32[4,512]{1,0:T(4,128)S(1)} %get-tuple-element.172, f32[4,512]{1,0:T(4,128)S(1)} %log_add_fusion), kind=kLoop, calls=%fused_computation.2 | loop fusion | flops 16777216 | bytes 41959424 | tf_op jit(solution)/shard_map/while/body/eval_jaxpr/convert_element_type | solution.py:256
  629.0 6.3 fusion.29
  635.4 4.9 multiply_bitcast_fusion
  651.4 121.1 %collective-permute-done.46 = bf16[256,2048]{1,0:T(8,128)(2,1)S(1)} collective-permute-done((bf16[256,2048]{1,0:T(8,128)(2,1)S(1)}, bf16[256,2048]{1,0:T(8,128)(2,1)S(1)}, u32[]{:S(2)}, u32[]{:S(2)}) %collective-permute-start.46) | collective-permute-done | bytes 1048608 | tf_op jit(solution)/shard_map/ppermute | solution.py:15
  774.2 20.8 %collective-permute-done.36 = bf16[1024,512]{0,1:T(8,128)(2,1)S(1)} collective-permute-done((bf16[1024,512]{0,1:T(8,128)(2,1)S(1)}, bf16[1024,512]{0,1:T(8,128)(2,1)S(1)}, u32[]{:S(2)}, u32[]{:S(2)}) %collective-permute-start.36) | collective-permute-done | bytes 1048608 | tf_op jit(solution)/shard_map/ppermute | solution.py:15
  795.0 12.9 collective-permute-start.47
  809.3 8.2 collective-permute-done.34
  817.5 12.9 collective-permute-start.37
  833.0 7.0 collective-permute-done.40
  840.0 6.7 collective-permute-start.35
  848.4 4.9 convert_add_fusion.1
  862.3 3.7 fusion.63
  870.5 3.7 fusion.59
  882.8 4.6 copy-done.1
  897.2 16.3 %collective-permute-done.42 = bf16[2048,256]{1,0:T(8,128)(2,1)} collective-permute-done((bf16[2048,256]{1,0:T(8,128)(2,1)}, bf16[2048,256]{1,0:T(8,128)(2,1)}, u32[]{:S(2)}, u32[]{:S(2)}) %collective-permute-start.42) | collective-permute-done | bytes 1048608 | tf_op jit(solution)/shard_map/ppermute | solution.py:15
  917.7 11.7 convert_add_fusion
  931.4 5.2 select_convert_fusion.3
  936.7 6.7 add_convert_fusion.1
  943.4 18.8 %collective-permute-done.38 = bf16[256,6144]{1,0:T(8,128)(2,1)} collective-permute-done((bf16[256,6144]{1,0:T(8,128)(2,1)}, bf16[256,6144]{1,0:T(8,128)(2,1)}, u32[]{:S(2)}, u32[]{:S(2)}) %collective-permute-start.38) | collective-permute-done | bytes 3145760 | tf_op jit(solution)/shard_map/ppermute | solution.py:15
  962.2 7.4 convert_add_fusion.2
  976.9 29.3 %reduce-scatter.7.cloned.1.call-done = bf16[256,128]{1,0:T(8,128)(2,1)} async-done(((bf16[2048,128]{1,0:T(8,128)(2,1)}), bf16[256,128]{1,0:T(8,128)(2,1)}) %reduce-scatter.7.cloned.1.call-update) | async-done | bytes 65552 | tf_op jit(solution)/shard_map/reduce_scatter | solution.py:323
  1007.8 6.0 add_convert_fusion
  1014.0 65.8 %reduce-scatter.11.cloned.1.call-done = bf16[256,128]{1,0:T(8,128)(2,1)} async-done(((bf16[2048,128]{1,0:T(8,128)(2,1)}), bf16[256,128]{1,0:T(8,128)(2,1)}) %reduce-scatter.11.cloned.1.call-update) | async-done | bytes 65552 | tf_op jit(solution)/shard_map/reduce_scatter | solution.py:329
  1081.3 71.9 %reduce-scatter.9.cloned.1.call-done = bf16[256,128]{1,0:T(8,128)(2,1)} async-done(((bf16[2048,128]{1,0:T(8,128)(2,1)}), bf16[256,128]{1,0:T(8,128)(2,1)}) %reduce-scatter.9.cloned.1.call-update) | async-done | bytes 65552 | tf_op jit(solution)/shard_map/reduce_scatter | solution.py:326
  1154.8 3.9 convert_add_fusion.3
  1164.7 17.9 %fusion.113 = (f32[4,17]{1,0:T(4,128)S(1)}, f32[128,4,17]{2,1,0:T(4,128)S(1)}) fusion(bf16[17,128,2048]{2,1,0:T(8,128)(2,1)S(1)} %bitcast.136, f32[128,2048,4]{1,0,2:T(8,128)S(1)} %add_bitcast_fusion), kind=kOutput, calls=%fused_computation.270 | convolution fusion | flops 213918144 | bytes 13142288 | tf_op jit(solution)/shard_map/transpose(jvp(tkj,jtd->ktd))/dot_general | solution.py:35
  1190.6 25.6 %fusion = bf16[17,128,2048]{2,0,1:T(8,128)(2,1)} fusion(f32[1,128,2048]{2,0,1:T(1,128)S(1)} %broadcast_in_dim.111, f32[128,4,17]{2,1,0:T(4,128)S(1)} %copy-done.33, f32[128,2048,4]{1,0,2:T(8,128)} %copy-done.25), kind=kOutput, calls=%fused_computation.1 | convolution fusion | flops 222822400 | bytes 14190592 | tf_op jit(solution)/shard_map/transpose(jvp(tkj,jtd->ktd))/dot_general | solution.py:35
  1216.2 13.6 %copy.76 = bf16[17,128,2048]{2,1,0:T(8,128)(2,1)} copy(bf16[17,128,2048]{2,0,1:T(8,128)(2,1)} %fusion) | data formatting | bytes 17825792
  1230.1 69.4 %all-reduce.5 = (f32[2048]{0:T(1024)}, f32[68,68]{1,0:T(8,128)}, f32[68]{0:T(128)}, f32[2048]{0:T(1024)}, f32[2048]{0:T(1024)}, /*index=5*/f32[2048]{0:T(1024)}, f32[2048]{0:T(1024)}) all-reduce(f32[2048]{0:T(1024)S(1)} %get-tuple-element.133, f32[68,68]{1,0:T(8,128)S(1)} %fusion.72, ...), channel_id=1, replica_groups=mesh['dp'=8,'tensor'=16] {'dp','tensor'}, use_global_device_ids=true, to_apply=%region_17.18 | all-reduce | flops 14932 | bytes 119456 | tf_op jit(solution)/shard_map/psum | solution.py:309
  1301.3 8.9 reduce-scatter.17.cloned.1.call-done
  1312.0 27.4 %all-reduce.8.cloned.1.call-done = f32[2048,68]{0,1:T(8,128)} async-done(((f32[2048,68]{0,1:T(8,128)}), f32[2048,68]{0,1:T(8,128)}) %all-reduce.8.cloned.1.call-update) | async-done | bytes 557072 | tf_op jit(solution)/shard_map/psum | solution.py:309
  (424 shorter events, 188.5 us)
Async XLA Ops:
  8.0 967.4 %reduce-scatter.13.cloned.1.call-start = ((), (), s32[]{:S(2)}) async-start(), calls=%async_computation.10 | async-start | bytes 589824 | tf_op jit(solution)/shard_map/reduce_scatter | solution.py:332
  8.1 68.1 %collective-permute-start.8 = (bf16[2048,128]{1,0:T(8,128)(2,1)}, bf16[2048,128]{1,0:T(8,128)(2,1)}, u32[]{:S(2)}, u32[]{:S(2)}) collective-permute-start(bf16[2048,128]{1,0:T(8,128)(2,1)} %param.28), channel_id=1, source_target_pairs={{0,1},{1,0},{2,3},{3,2},{4,5},{5,4},{6,7},{7,6},{8,9},{9,8},{10,11... | collective-permute-start | bytes 1572872 | tf_op jit(solution)/shard_map/ppermute | solution.py:15
  9.6 37.6 %collective-permute-start.12 = (bf16[2048,128]{1,0:T(8,128)(2,1)}, bf16[2048,128]{1,0:T(8,128)(2,1)}, u32[]{:S(2)}, u32[]{:S(2)}) collective-permute-start(bf16[2048,128]{1,0:T(8,128)(2,1)} %param.29), channel_id=1, source_target_pairs={{0,1},{1,0},{2,3},{3,2},{4,5},{5,4},{6,7},{7,6},{8,9},{9,8},{10,11... | collective-permute-start | bytes 1572872 | tf_op jit(solution)/shard_map/ppermute | solution.py:15
  9.7 61.6 %collective-permute-start.2 = (bf16[2048,128]{1,0:T(8,128)(2,1)}, bf16[2048,128]{1,0:T(8,128)(2,1)}, u32[]{:S(2)}, u32[]{:S(2)}) collective-permute-start(bf16[2048,128]{1,0:T(8,128)(2,1)} %param.30), channel_id=1, source_target_pairs={{0,1},{1,0},{2,3},{3,2},{4,5},{5,4},{6,7},{7,6},{8,9},{9,8},{10,11... | collective-permute-start | bytes 1572872 | tf_op jit(solution)/shard_map/ppermute | solution.py:15
  40.5 37.9 %collective-permute-start = (bf16[128,2048]{1,0:T(8,128)(2,1)S(1)}, bf16[128,2048]{1,0:T(8,128)(2,1)}, u32[]{:S(2)}, u32[]{:S(2)}) collective-permute-start(bf16[128,2048]{1,0:T(8,128)(2,1)S(1)} %multiply_convert_fusion.5), channel_id=1, source_target_pairs={{0,4},{1,5},{2,6},{3,7},{4,0},{5,1},{6,2},{7,3},{8,12},{9,13},{10,... | collective-permute-start | bytes 1572872 | tf_op jit(solution)/shard_map/ppermute | solution.py:15
  44.9 22.5 %collective-permute-start.10 = (bf16[128,2048]{1,0:T(8,128)(2,1)S(1)}, bf16[128,2048]{1,0:T(8,128)(2,1)}, u32[]{:S(2)}, u32[]{:S(2)}) collective-permute-start(bf16[128,2048]{1,0:T(8,128)(2,1)S(1)} %multiply_convert_fusion.3), channel_id=1, source_target_pairs={{0,4},{1,5},{2,6},{3,7},{4,0},{5,1},{6,2},{7,3},{8,12},{9,13},{10,... | collective-permute-start | bytes 1572872 | tf_op jit(solution)/shard_map/ppermute | solution.py:15
  50.0 52.6 %collective-permute-start.13 = (bf16[2048,256]{1,0:T(8,128)(2,1)}, bf16[2048,256]{1,0:T(8,128)(2,1)}, u32[]{:S(2)}, u32[]{:S(2)}) collective-permute-start(bf16[2048,256]{1,0:T(8,128)(2,1)} %maximum_select_fusion.29), channel_id=1, source_target_pairs={{0,2},{1,3},{2,0},{3,1},{4,6},{5,7},{6,4},{7,5},{8,10},{9,11},{10,... | collective-permute-start | bytes 3145736 | tf_op jit(solution)/shard_map/ppermute | solution.py:15
  70.0 32.9 %collective-permute-start.11 = (bf16[256,2048]{1,0:T(8,128)(2,1)}, bf16[256,2048]{1,0:T(8,128)(2,1)}, u32[]{:S(2)}, u32[]{:S(2)}) collective-permute-start(bf16[256,2048]{1,0:T(8,128)(2,1)} %maximum_select_fusion.28), channel_id=1, source_target_pairs={{0,8},{1,9},{2,10},{3,11},{4,12},{5,13},{6,14},{7,15},{8,0},{9,1},... | collective-permute-start | bytes 3145736 | tf_op jit(solution)/shard_map/ppermute | solution.py:15
  71.3 29.7 %collective-permute-start.6 = (bf16[128,2048]{1,0:T(8,128)(2,1)S(1)}, bf16[128,2048]{1,0:T(8,128)(2,1)S(1)}, u32[]{:S(2)}, u32[]{:S(2)}) collective-permute-start(bf16[128,2048]{1,0:T(8,128)(2,1)S(1)} %multiply_convert_fusion.4), channel_id=1, source_target_pairs={{0,4},{1,5},{2,6},{3,7},{4,0},{5,1},{6,2},{7,3},{8,12},{9,13},{10,... | collective-permute-start | bytes 1572872 | tf_op jit(solution)/shard_map/ppermute | solution.py:15
  76.1 47.7 %collective-permute-start.3 = (bf16[2048,256]{1,0:T(8,128)(2,1)S(1)}, bf16[2048,256]{1,0:T(8,128)(2,1)S(1)}, u32[]{:S(2)}, u32[]{:S(2)}) collective-permute-start(bf16[2048,256]{1,0:T(8,128)(2,1)S(1)} %maximum_select_fusion.23), channel_id=1, source_target_pairs={{0,2},{1,3},{2,0},{3,1},{4,6},{5,7},{6,4},{7,5},{8,10},{9,11},{10,... | collective-permute-start | bytes 3145736 | tf_op jit(solution)/shard_map/ppermute | solution.py:15
  78.4 69.1 %copy-start.37 = (bf16[2048,256]{1,0:T(8,128)(2,1)}, bf16[2048,256]{1,0:T(8,128)(2,1)S(1)}, u32[]{:S(2)}) copy-start(bf16[2048,256]{1,0:T(8,128)(2,1)S(1)} %maximum_select_fusion.27) | copy-start | bytes 3145732
  78.5 67.9 %collective-permute-start.9 = (bf16[2048,256]{1,0:T(8,128)(2,1)S(1)}, bf16[2048,256]{1,0:T(8,128)(2,1)S(1)}, u32[]{:S(2)}, u32[]{:S(2)}) collective-permute-start(bf16[2048,256]{1,0:T(8,128)(2,1)S(1)} %maximum_select_fusion.27), channel_id=1, source_target_pairs={{0,2},{1,3},{2,0},{3,1},{4,6},{5,7},{6,4},{7,5},{8,10},{9,11},{10,... | collective-permute-start | bytes 3145736 | tf_op jit(solution)/shard_map/ppermute | solution.py:15
  101.0 24.2 %collective-permute-start.1 = (bf16[256,2048]{1,0:T(8,128)(2,1)S(1)}, bf16[256,2048]{1,0:T(8,128)(2,1)S(1)}, u32[]{:S(2)}, u32[]{:S(2)}) collective-permute-start(bf16[256,2048]{1,0:T(8,128)(2,1)S(1)} %maximum_select_fusion.22), channel_id=1, source_target_pairs={{0,8},{1,9},{2,10},{3,11},{4,12},{5,13},{6,14},{7,15},{8,0},{9,1},... | collective-permute-start | bytes 3145736 | tf_op jit(solution)/shard_map/ppermute | solution.py:15
  102.6 45.0 %collective-permute-start.7 = (bf16[256,2048]{1,0:T(8,128)(2,1)S(1)}, bf16[256,2048]{1,0:T(8,128)(2,1)S(1)}, u32[]{:S(2)}, u32[]{:S(2)}) collective-permute-start(bf16[256,2048]{1,0:T(8,128)(2,1)S(1)} %maximum_select_fusion.26), channel_id=1, source_target_pairs={{0,8},{1,9},{2,10},{3,11},{4,12},{5,13},{6,14},{7,15},{8,0},{9,1},... | collective-permute-start | bytes 3145736 | tf_op jit(solution)/shard_map/ppermute | solution.py:15
  107.9 21.9 %collective-permute-start.14 = (bf16[512,512]{0,1:T(8,128)(2,1)S(1)}, bf16[512,512]{0,1:T(8,128)(2,1)S(1)}, u32[]{:S(2)}, u32[]{:S(2)}) collective-permute-start(bf16[512,512]{0,1:T(8,128)(2,1)S(1)} %convolution_convert_fusion.1), channel_id=1, source_target_pairs={{0,1},{1,0},{2,3},{3,2},{4,5},{5,4},{6,7},{7,6},{8,9},{9,8},{10,11... | collective-permute-start | bytes 1572872 | tf_op jit(solution)/shard_map/ppermute | solution.py:15
  123.9 6.3 collective-permute-start.16
  125.2 102.2 %collective-permute-start.22 = (bf16[2048,512]{1,0:T(8,128)(2,1)}, bf16[2048,512]{1,0:T(8,128)(2,1)}, u32[]{:S(2)}, u32[]{:S(2)}) collective-permute-start(bf16[2048,512]{1,0:T(8,128)(2,1)} %param.32), channel_id=1, source_target_pairs={{0,1},{1,0},{2,3},{3,2},{4,5},{5,4},{6,7},{7,6},{8,9},{9,8},{10,11... | collective-permute-start | bytes 6291464 | tf_op jit(solution)/shard_map/ppermute | solution.py:15
  129.8 19.2 %collective-permute-start.4 = (bf16[512,512]{0,1:T(8,128)(2,1)S(1)}, bf16[512,512]{0,1:T(8,128)(2,1)S(1)}, u32[]{:S(2)}, u32[]{:S(2)}) collective-permute-start(bf16[512,512]{0,1:T(8,128)(2,1)S(1)} %convolution_convert_fusion.3), channel_id=1, source_target_pairs={{0,1},{1,0},{2,3},{3,2},{4,5},{5,4},{6,7},{7,6},{8,9},{9,8},{10,11... | collective-permute-start | bytes 1572872 | tf_op jit(solution)/shard_map/ppermute | solution.py:15
  130.2 38.6 %collective-permute-start.15 = (bf16[1024,512]{0,1:T(8,128)(2,1)S(1)}, bf16[1024,512]{0,1:T(8,128)(2,1)S(1)}, u32[]{:S(2)}, u32[]{:S(2)}) collective-permute-start(bf16[1024,512]{0,1:T(8,128)(2,1)S(1)} %maximum_select_fusion.30), channel_id=1, source_target_pairs={{0,2},{1,3},{2,0},{3,1},{4,6},{5,7},{6,4},{7,5},{8,10},{9,11},{10,... | collective-permute-start | bytes 3145736 | tf_op jit(solution)/shard_map/ppermute | solution.py:15
  146.4 75.9 %collective-permute-start.17 = (bf16[256,2048]{1,0:T(8,128)(2,1)}, bf16[256,2048]{1,0:T(8,128)(2,1)}, u32[]{:S(2)}, u32[]{:S(2)}) collective-permute-start(bf16[256,2048]{1,0:T(8,128)(2,1)} %maximum_select_fusion.32), channel_id=1, source_target_pairs={{0,2},{1,3},{2,0},{3,1},{4,6},{5,7},{6,4},{7,5},{8,10},{9,11},{10,... | collective-permute-start | bytes 3145736 | tf_op jit(solution)/shard_map/ppermute | solution.py:15
  150.2 63.7 %collective-permute-start.5 = (bf16[1024,512]{0,1:T(8,128)(2,1)}, bf16[1024,512]{0,1:T(8,128)(2,1)}, u32[]{:S(2)}, u32[]{:S(2)}) collective-permute-start(bf16[1024,512]{0,1:T(8,128)(2,1)} %maximum_select_fusion.24), channel_id=1, source_target_pairs={{0,2},{1,3},{2,0},{3,1},{4,6},{5,7},{6,4},{7,5},{8,10},{9,11},{10,... | collective-permute-start | bytes 3145736 | tf_op jit(solution)/shard_map/ppermute | solution.py:15
  226.1 23.9 %collective-permute-start.18 = (bf16[256,2048]{1,0:T(8,128)(2,1)S(1)}, bf16[256,2048]{1,0:T(8,128)(2,1)S(1)}, u32[]{:S(2)}, u32[]{:S(2)}) collective-permute-start(bf16[256,2048]{1,0:T(8,128)(2,1)S(1)} %select_convert_fusion.14), channel_id=1, source_target_pairs={{0,8},{1,9},{2,10},{3,11},{4,12},{5,13},{6,14},{7,15},{8,0},{9,1},... | collective-permute-start | bytes 3145736 | tf_op jit(solution)/shard_map/ppermute | solution.py:15
  232.5 131.4 %collective-permute-start.23 = (bf16[2048,1024]{1,0:T(8,128)(2,1)S(1)}, bf16[2048,1024]{1,0:T(8,128)(2,1)S(1)}, u32[]{:S(2)}, u32[]{:S(2)}) collective-permute-start(bf16[2048,1024]{1,0:T(8,128)(2,1)S(1)} %maximum_select_fusion.2), channel_id=1, source_target_pairs={{0,2},{1,3},{2,0},{3,1},{4,6},{5,7},{6,4},{7,5},{8,10},{9,11},{10,... | collective-permute-start | bytes 12582920 | tf_op jit(solution)/shard_map/ppermute | solution.py:15
  250.5 85.5 %copy-start.51 = (f32[2048]{0:T(1024)S(1)}, f32[2048]{0:T(1024)}, u32[]{:S(2)}) copy-start(f32[2048]{0:T(1024)} %param.27) | copy-start | bytes 24580
  250.6 84.5 %collective-permute-start.19 = (bf16[128,2048]{1,0:T(8,128)(2,1)S(1)}, bf16[128,2048]{1,0:T(8,128)(2,1)S(1)}, u32[]{:S(2)}, u32[]{:S(2)}) collective-permute-start(bf16[128,2048]{1,0:T(8,128)(2,1)S(1)} %select_convert_fusion.23), channel_id=1, source_target_pairs={{0,4},{1,5},{2,6},{3,7},{4,0},{5,1},{6,2},{7,3},{8,12},{9,13},{10,... | collective-permute-start | bytes 1572872 | tf_op jit(solution)/shard_map/ppermute | solution.py:15
  252.2 99.6 %collective-permute-start.24 = (bf16[512,2048]{1,0:T(8,128)(2,1)S(1)}, bf16[512,2048]{1,0:T(8,128)(2,1)S(1)}, u32[]{:S(2)}, u32[]{:S(2)}) collective-permute-start(bf16[512,2048]{1,0:T(8,128)(2,1)S(1)} %copy-done.31), channel_id=1, source_target_pairs={{0,1},{1,0},{2,3},{3,2},{4,5},{5,4},{6,7},{7,6},{8,9},{9,8},{10,11... | collective-permute-start | bytes 6291464 | tf_op jit(solution)/shard_map/ppermute | solution.py:15
  336.2 13.2 collective-permute-start.20
  349.7 22.1 %collective-permute-start.21 = (bf16[256,2048]{1,0:T(8,128)(2,1)S(1)}, bf16[256,2048]{1,0:T(8,128)(2,1)}, u32[]{:S(2)}, u32[]{:S(2)}) collective-permute-start(bf16[256,2048]{1,0:T(8,128)(2,1)S(1)} %maximum_select_fusion.33), channel_id=1, source_target_pairs={{0,8},{1,9},{2,10},{3,11},{4,12},{5,13},{6,14},{7,15},{8,0},{9,1},... | collective-permute-start | bytes 3145736 | tf_op jit(solution)/shard_map/ppermute | solution.py:15
  350.0 11.9 collective-permute-start.28
  355.6 95.4 %collective-permute-start.25 = (bf16[1024,2048]{1,0:T(8,128)(2,1)}, bf16[1024,2048]{1,0:T(8,128)(2,1)}, u32[]{:S(2)}, u32[]{:S(2)}) collective-permute-start(bf16[1024,2048]{1,0:T(8,128)(2,1)} %maximum_select_fusion.3), channel_id=1, source_target_pairs={{0,2},{1,3},{2,0},{3,1},{4,6},{5,7},{6,4},{7,5},{8,10},{9,11},{10,... | collective-permute-start | bytes 12582920 | tf_op jit(solution)/shard_map/ppermute | solution.py:15
  362.2 88.8 %copy-start.43 = (bf16[256,2048]{1,0:T(8,128)(2,1)}, bf16[256,2048]{1,0:T(8,128)(2,1)S(1)}, u32[]{:S(2)}) copy-start(bf16[256,2048]{1,0:T(8,128)(2,1)S(1)} %maximum_select_fusion.34) | copy-start | bytes 3145732
  362.2 35.9 %collective-permute-start.29 = (bf16[256,2048]{1,0:T(8,128)(2,1)S(1)}, bf16[256,2048]{1,0:T(8,128)(2,1)}, u32[]{:S(2)}, u32[]{:S(2)}) collective-permute-start(bf16[256,2048]{1,0:T(8,128)(2,1)S(1)} %maximum_select_fusion.34), channel_id=1, source_target_pairs={{0,8},{1,9},{2,10},{3,11},{4,12},{5,13},{6,14},{7,15},{8,0},{9,1},... | collective-permute-start | bytes 3145736 | tf_op jit(solution)/shard_map/ppermute | solution.py:15
  492.6 47.8 %collective-permute-start.26 = (bf16[256,2048]{1,0:T(8,128)(2,1)S(1)}, bf16[256,2048]{1,0:T(8,128)(2,1)}, u32[]{:S(2)}, u32[]{:S(2)}) collective-permute-start(bf16[256,2048]{1,0:T(8,128)(2,1)S(1)} %select_convert_fusion.13), channel_id=1, source_target_pairs={{0,8},{1,9},{2,10},{3,11},{4,12},{5,13},{6,14},{7,15},{8,0},{9,1},... | collective-permute-start | bytes 3145736 | tf_op jit(solution)/shard_map/ppermute | solution.py:15
  493.9 41.8 %collective-permute-start.30 = (bf16[256,2048]{1,0:T(8,128)(2,1)S(1)}, bf16[256,2048]{1,0:T(8,128)(2,1)}, u32[]{:S(2)}, u32[]{:S(2)}) collective-permute-start(bf16[256,2048]{1,0:T(8,128)(2,1)S(1)} %select_convert_fusion.12), channel_id=1, source_target_pairs={{0,8},{1,9},{2,10},{3,11},{4,12},{5,13},{6,14},{7,15},{8,0},{9,1},... | collective-permute-start | bytes 3145736 | tf_op jit(solution)/shard_map/ppermute | solution.py:15
  538.8 9.6 collective-permute-start.31
  542.3 17.6 %collective-permute-start.27 = (bf16[128,2048]{1,0:T(8,128)(2,1)S(1)}, bf16[128,2048]{1,0:T(8,128)(2,1)S(1)}, u32[]{:S(2)}, u32[]{:S(2)}) collective-permute-start(bf16[128,2048]{1,0:T(8,128)(2,1)S(1)} %select_convert_fusion.22), channel_id=1, source_target_pairs={{0,4},{1,5},{2,6},{3,7},{4,0},{5,1},{6,2},{7,3},{8,12},{9,13},{10,... | collective-permute-start | bytes 1572872 | tf_op jit(solution)/shard_map/ppermute | solution.py:15
  561.7 9.5 collective-permute-start.32
  565.6 281.5 %collective-permute-start.48 = (bf16[2048,1024]{1,0:T(8,128)(2,1)}, bf16[2048,1024]{1,0:T(8,128)(2,1)}, u32[]{:S(2)}, u32[]{:S(2)}) collective-permute-start(bf16[2048,1024]{1,0:T(8,128)(2,1)} %select_convert_fusion.1), channel_id=1, source_target_pairs={{0,2},{1,3},{2,0},{3,1},{4,6},{5,7},{6,4},{7,5},{8,10},{9,11},{10,... | collective-permute-start | bytes 12582920 | tf_op jit(solution)/shard_map/ppermute | solution.py:15
  571.6 18.2 %collective-permute-start.33 = (bf16[256,2048]{1,0:T(8,128)(2,1)S(1)}, bf16[256,2048]{1,0:T(8,128)(2,1)S(1)}, u32[]{:S(2)}, u32[]{:S(2)}) collective-permute-start(bf16[256,2048]{1,0:T(8,128)(2,1)S(1)} %maximum_select_fusion.35), channel_id=1, source_target_pairs={{0,8},{1,9},{2,10},{3,11},{4,12},{5,13},{6,14},{7,15},{8,0},{9,1},... | collective-permute-start | bytes 3145736 | tf_op jit(solution)/shard_map/ppermute | solution.py:15
  588.3 329.4 %collective-permute-start.50 = (bf16[1024,2048]{1,0:T(8,128)(2,1)}, bf16[1024,2048]{1,0:T(8,128)(2,1)}, u32[]{:S(2)}, u32[]{:S(2)}) collective-permute-start(bf16[1024,2048]{1,0:T(8,128)(2,1)} %select_convert_fusion), channel_id=1, source_target_pairs={{0,2},{1,3},{2,0},{3,1},{4,6},{5,7},{6,4},{7,5},{8,10},{9,11},{10,... | collective-permute-start | bytes 12582920 | tf_op jit(solution)/shard_map/ppermute | solution.py:15
  642.1 130.5 %collective-permute-start.46 = (bf16[256,2048]{1,0:T(8,128)(2,1)S(1)}, bf16[256,2048]{1,0:T(8,128)(2,1)S(1)}, u32[]{:S(2)}, u32[]{:S(2)}) collective-permute-start(bf16[256,2048]{1,0:T(8,128)(2,1)S(1)} %select_convert_fusion.6), channel_id=1, source_target_pairs={{0,2},{1,3},{2,0},{3,1},{4,6},{5,7},{6,4},{7,5},{8,10},{9,11},{10,... | collective-permute-start | bytes 3145736 | tf_op jit(solution)/shard_map/ppermute | solution.py:15
  643.4 151.7 %collective-permute-start.36 = (bf16[1024,512]{0,1:T(8,128)(2,1)S(1)}, bf16[1024,512]{0,1:T(8,128)(2,1)S(1)}, u32[]{:S(2)}, u32[]{:S(2)}) collective-permute-start(bf16[1024,512]{0,1:T(8,128)(2,1)S(1)} %bitcast.146), channel_id=1, source_target_pairs={{0,2},{1,3},{2,0},{3,1},{4,6},{5,7},{6,4},{7,5},{8,10},{9,11},{10,... | collective-permute-start | bytes 3145736 | tf_op jit(solution)/shard_map/ppermute | solution.py:15
  644.1 173.4 %collective-permute-start.34 = (bf16[1024,512]{0,1:T(8,128)(2,1)S(1)}, bf16[1024,512]{0,1:T(8,128)(2,1)S(1)}, u32[]{:S(2)}, u32[]{:S(2)}) collective-permute-start(bf16[1024,512]{0,1:T(8,128)(2,1)S(1)} %bitcast.145), channel_id=1, source_target_pairs={{0,2},{1,3},{2,0},{3,1},{4,6},{5,7},{6,4},{7,5},{8,10},{9,11},{10,... | collective-permute-start | bytes 3145736 | tf_op jit(solution)/shard_map/ppermute | solution.py:15
  772.6 67.4 %collective-permute-start.40 = (bf16[2048,256]{1,0:T(8,128)(2,1)S(1)}, bf16[2048,256]{1,0:T(8,128)(2,1)S(1)}, u32[]{:S(2)}, u32[]{:S(2)}) collective-permute-start(bf16[2048,256]{1,0:T(8,128)(2,1)S(1)} %select_convert_fusion.9), channel_id=1, source_target_pairs={{0,2},{1,3},{2,0},{3,1},{4,6},{5,7},{6,4},{7,5},{8,10},{9,11},{10,... | collective-permute-start | bytes 3145736 | tf_op jit(solution)/shard_map/ppermute | solution.py:15
  772.8 75.5 %slice-start.7 = ((s8[16777216]{0:T(1024)(128)(4,1)}), s8[4194304]{0:T(1024)(128)(4,1)S(1)}, s32[]{:S(2)}) async-start(s8[16777216]{0:T(1024)(128)(4,1)} %bitcast.137), calls=%async_computation.20 | async-start | bytes 8388608
  773.3 75.0 %slice-start.8 = ((s8[16777216]{0:T(1024)(128)(4,1)}), s8[4194304]{0:T(1024)(128)(4,1)S(1)}, s32[]{:S(2)}) async-start(s8[16777216]{0:T(1024)(128)(4,1)} %bitcast.137), calls=%async_computation.21 | async-start | bytes 8388608
  795.0 63.3 %collective-permute-start.47 = (bf16[128,2048]{1,0:T(8,128)(2,1)}, bf16[128,2048]{1,0:T(8,128)(2,1)}, u32[]{:S(2)}, u32[]{:S(2)}) collective-permute-start(bf16[128,2048]{1,0:T(8,128)(2,1)} %select_convert_fusion.15), channel_id=1, source_target_pairs={{0,1},{1,0},{2,3},{3,2},{4,5},{5,4},{6,7},{7,6},{8,9},{9,8},{10,11... | collective-permute-start | bytes 1572872 | tf_op jit(solution)/shard_map/ppermute | solution.py:15
  817.5 43.5 %collective-permute-start.37 = (bf16[512,512]{0,1:T(8,128)(2,1)}, bf16[512,512]{0,1:T(8,128)(2,1)}, u32[]{:S(2)}, u32[]{:S(2)}) collective-permute-start(bf16[512,512]{0,1:T(8,128)(2,1)} %select_convert_fusion.19), channel_id=1, source_target_pairs={{0,1},{1,0},{2,3},{3,2},{4,5},{5,4},{6,7},{7,6},{8,9},{9,8},{10,11... | collective-permute-start | bytes 1572872 | tf_op jit(solution)/shard_map/ppermute | solution.py:15
  840.0 27.3 %collective-permute-start.35 = (bf16[512,512]{0,1:T(8,128)(2,1)}, bf16[512,512]{0,1:T(8,128)(2,1)}, u32[]{:S(2)}, u32[]{:S(2)}) collective-permute-start(bf16[512,512]{0,1:T(8,128)(2,1)} %select_convert_fusion.20), channel_id=1, source_target_pairs={{0,1},{1,0},{2,3},{3,2},{4,5},{5,4},{6,7},{7,6},{8,9},{9,8},{10,11... | collective-permute-start | bytes 1572872 | tf_op jit(solution)/shard_map/ppermute | solution.py:15
  848.3 41.2 %collective-permute-start.41 = (bf16[2048,128]{1,0:T(8,128)(2,1)S(1)}, bf16[2048,128]{1,0:T(8,128)(2,1)}, u32[]{:S(2)}, u32[]{:S(2)}) collective-permute-start(bf16[2048,128]{1,0:T(8,128)(2,1)S(1)} %select_convert_fusion.18), channel_id=1, source_target_pairs={{0,1},{1,0},{2,3},{3,2},{4,5},{5,4},{6,7},{7,6},{8,9},{9,8},{10,11... | collective-permute-start | bytes 1572872 | tf_op jit(solution)/shard_map/ppermute | solution.py:15
  858.3 78.3 %collective-permute-start.49 = (bf16[2048,512]{1,0:T(8,128)(2,1)}, bf16[2048,512]{1,0:T(8,128)(2,1)}, u32[]{:S(2)}, u32[]{:S(2)}) collective-permute-start(bf16[2048,512]{1,0:T(8,128)(2,1)} %select_convert_fusion.4), channel_id=1, source_target_pairs={{0,1},{1,0},{2,3},{3,2},{4,5},{5,4},{6,7},{7,6},{8,9},{9,8},{10,11... | collective-permute-start | bytes 6291464 | tf_op jit(solution)/shard_map/ppermute | solution.py:15
  860.9 145.3 %reduce-scatter.7.cloned.1.call-start = ((), (), s32[]{:S(2)}) async-start(), calls=%async_computation.7 | async-start | bytes 589824 | tf_op jit(solution)/shard_map/reduce_scatter | solution.py:323
  866.2 26.7 %collective-permute-start.44 = (bf16[2048,256]{1,0:T(8,128)(2,1)S(1)}, bf16[2048,256]{1,0:T(8,128)(2,1)}, u32[]{:S(2)}, u32[]{:S(2)}) collective-permute-start(bf16[2048,256]{1,0:T(8,128)(2,1)S(1)} %select_convert_fusion.7), channel_id=1, source_target_pairs={{0,2},{1,3},{2,0},{3,1},{4,6},{5,7},{6,4},{7,5},{8,10},{9,11},{10,... | collective-permute-start | bytes 3145736 | tf_op jit(solution)/shard_map/ppermute | solution.py:15
  875.6 38.0 %collective-permute-start.42 = (bf16[2048,256]{1,0:T(8,128)(2,1)}, bf16[2048,256]{1,0:T(8,128)(2,1)}, u32[]{:S(2)}, u32[]{:S(2)}) collective-permute-start(bf16[2048,256]{1,0:T(8,128)(2,1)} %select_convert_fusion.8), channel_id=1, source_target_pairs={{0,2},{1,3},{2,0},{3,1},{4,6},{5,7},{6,4},{7,5},{8,10},{9,11},{10,... | collective-permute-start | bytes 3145736 | tf_op jit(solution)/shard_map/ppermute | solution.py:15
  889.5 72.7 %collective-permute-start.38 = (bf16[256,6144]{1,0:T(8,128)(2,1)}, bf16[256,6144]{1,0:T(8,128)(2,1)}, u32[]{:S(2)}, u32[]{:S(2)}) collective-permute-start(bf16[256,6144]{1,0:T(8,128)(2,1)} %select_convert_fusion.2), channel_id=1, source_target_pairs={{0,8},{1,9},{2,10},{3,11},{4,12},{5,13},{6,14},{7,15},{8,0},{9,1},... | collective-permute-start | bytes 9437192 | tf_op jit(solution)/shard_map/ppermute | solution.py:15
  892.9 186.9 %reduce-scatter.11.cloned.1.call-start = ((), (), s32[]{:S(2)}) async-start(), calls=%async_computation.9 | async-start | bytes 589824 | tf_op jit(solution)/shard_map/reduce_scatter | solution.py:329
  896.1 20.6 %collective-permute-start.45 = (bf16[2048,128]{1,0:T(8,128)(2,1)S(1)}, bf16[2048,128]{1,0:T(8,128)(2,1)S(1)}, u32[]{:S(2)}, u32[]{:S(2)}) collective-permute-start(bf16[2048,128]{1,0:T(8,128)(2,1)S(1)} %select_convert_fusion.16), channel_id=1, source_target_pairs={{0,1},{1,0},{2,3},{3,2},{4,5},{5,4},{6,7},{7,6},{8,9},{9,8},{10,11... | collective-permute-start | bytes 1572872 | tf_op jit(solution)/shard_map/ppermute | solution.py:15
  915.3 14.1 %collective-permute-start.43 = (bf16[2048,128]{1,0:T(8,128)(2,1)S(1)}, bf16[2048,128]{1,0:T(8,128)(2,1)}, u32[]{:S(2)}, u32[]{:S(2)}) collective-permute-start(bf16[2048,128]{1,0:T(8,128)(2,1)S(1)} %select_convert_fusion.17), channel_id=1, source_target_pairs={{0,1},{1,0},{2,3},{3,2},{4,5},{5,4},{6,7},{7,6},{8,9},{9,8},{10,11... | collective-permute-start | bytes 1572872 | tf_op jit(solution)/shard_map/ppermute | solution.py:15
  917.7 235.6 %reduce-scatter.9.cloned.1.call-start = ((), (), s32[]{:S(2)}) async-start(), calls=%async_computation.8 | async-start | bytes 589824 | tf_op jit(solution)/shard_map/reduce_scatter | solution.py:326
  931.4 368.1 %reduce-scatter.15.cloned.1.call-start = ((), (), s32[]{:S(2)}) async-start(), calls=%async_computation.11 | async-start | bytes 2359296 | tf_op jit(solution)/shard_map/reduce_scatter | solution.py:335
  936.6 71.1 %collective-permute-start.51 = (bf16[512,2048]{1,0:T(8,128)(2,1)}, bf16[512,2048]{1,0:T(8,128)(2,1)S(1)}, u32[]{:S(2)}, u32[]{:S(2)}) collective-permute-start(bf16[512,2048]{1,0:T(8,128)(2,1)} %select_convert_fusion.3), channel_id=1, source_target_pairs={{0,1},{1,0},{2,3},{3,2},{4,5},{5,4},{6,7},{7,6},{8,9},{9,8},{10,11... | collective-permute-start | bytes 6291464 | tf_op jit(solution)/shard_map/ppermute | solution.py:15
  943.3 366.9 %reduce-scatter.17.cloned.1.call-start = ((), (), s32[]{:S(2)}) async-start(), calls=%async_computation.12 | async-start | bytes 2359296 | tf_op jit(solution)/shard_map/reduce_scatter | solution.py:338
  973.8 181.0 %collective-permute-start.39 = (bf16[128,6144]{1,0:T(8,128)(2,1)}, bf16[128,6144]{1,0:T(8,128)(2,1)}, u32[]{:S(2)}, u32[]{:S(2)}) collective-permute-start(bf16[128,6144]{1,0:T(8,128)(2,1)} %select_convert_fusion.5), channel_id=1, source_target_pairs={{0,4},{1,5},{2,6},{3,7},{4,0},{5,1},{6,2},{7,3},{8,12},{9,13},{10,... | collective-permute-start | bytes 4718600 | tf_op jit(solution)/shard_map/ppermute | solution.py:15
  1013.8 325.6 %all-reduce.8.cloned.1.call-start = ((), (), s32[]{:S(2)}) async-start(), calls=%async_computation.6 | async-start | bytes 1179648 | tf_op jit(solution)/shard_map/psum | solution.py:309
  (100 other events, 1016.6 us)
Sparse Core Ops, SparseCore 0:
  861.0 71.6 reduce-scatter.12
  936.8 69.4 reduce-scatter.6
  1010.8 68.9 reduce-scatter.10
  1083.8 69.4 reduce-scatter.8
  1157.3 74.6 reduce-scatter.14
  1235.9 74.2 reduce-scatter.16
Sparse Core Ops, SparseCore 1:
  1190.6 148.7 all-reduce.7
where the time goes:
time: 1350 us
  waiting for transfers between devices  731 us (54%)
  matrix products  235 us (17%)
  other arithmetic  157 us (12%)
  starting transfers between devices  90.5 us (7%)
  blocking collectives  69.4 us (5%)
  local copies, waits for them, and re-layouts  49.2 us (4%)
  between operations  17.8 us (1%)
    ppermute x52, waiting for transfers between devices, swapped(): lax.ppermute(x, axis, [(i, i ^ 1 << bit) for i in range(lax.axis_size(axi...  528 us
    ppermute x52, starting transfers between devices, swapped(): lax.ppermute(x, axis, [(i, i ^ 1 << bit) for i in range(lax.axis_size(axi...  90.1 us
    reduce_scatter x1, waiting for transfers between devices, on_device(): lax.psum_scatter(grad_w_key.astype(jnp.bfloat16), 'dp', scatter_dimension...  71.9 us
    psum x1, blocking collectives, on_device(): lax.psum((front_grads[1], front_grads[2], front_grads[3], front_grads[4],...  69.4 us
    reduce_scatter x1, waiting for transfers between devices, on_device(): lax.psum_scatter(grad_w_value.astype(jnp.bfloat16), 'dp', scatter_dimensi...  65.8 us
    dot_general x3, matrix products, front_part(): jnp.einsum('tkj,jtd->ktd', mixing, history_float, precision=PRECISE)  63.3 us
    unnamed x212, local copies, waits for them, and re-layouts  44.7 us
    dot_general x6, matrix products, across_cols(): lax.dot_general(left_side, right_side, (((1,), (1,)), ((), ())), preferre...  43.8 us
  transfers between devices with their start and end apart: 59, of which 27 were waited for; matrix products, arithmetic and copies ran while one was open for 27% of the time, Pallas kernels for 0%

commit v1 on v0

--- a/solution.py
+++ b/solution.py
@@ -306,7 +306,7 @@
         )
     )
     grad_history = front_grads[0].astype(jnp.bfloat16)
-    small_sums = lax.psum(
+    partial = lax.psum(
         (
             front_grads[1],
             front_grads[2],
@@ -317,8 +317,9 @@
             front_grads[7],
             grad_gain_mlp,
         ),
-        ("dp", "tensor"),
-    )
+        "dp",
+    )
+    small_sums = lax.psum(partial, "tensor")
     sum_query, sum_key, sum_value, sum_output, sum_expand, sum_reduce = (
         lax.psum_scatter(
             grad_w_query.astype(jnp.bfloat16), "dp", scatter_dimension=0, tiled=True

time: 1350 us -> 1520 us (1.13)
  waiting for transfers between devices: 731 us -> 884 us
  blocking collectives: 69.4 us -> 95 us
    psum x0 -> x1, waiting for transfers between devices: none -> 116 us  [on_device(): small_sums = lax.psum(partial, 'tensor')]
    psum x0 -> x1, blocking collectives: none -> 63 us  [on_device(): small_sums = lax.psum(partial, 'tensor')]
    psum x1, waiting for transfers between devices: 27.4 us -> 78.7 us  [on_device(): lax.psum((front_grads[1], front_grads[2], front_grads[3], front_grads[4],...]
    ppermute x52, waiting for transfers between devices: 528 us -> 578 us  [swapped(): lax.ppermute(x, axis, [(i, i ^ 1 << bit) for i in range(lax.axis_size(axi...]
    reduce_scatter x1, waiting for transfers between devices: 65.8 us -> 16.9 us  [on_device(): lax.psum_scatter(grad_w_value.astype(jnp.bfloat16), 'dp', scatter_dimensi...]
    psum x1, blocking collectives: 69.4 us -> 31.9 us  [on_device(): lax.psum((front_grads[1], front_grads[2], front_grads[3], front_grads[4],...]
    reduce_scatter x1, waiting for transfers between devices: 29.3 us -> 0.01 us  [on_device(): lax.psum_scatter(grad_w_query.astype(jnp.bfloat16), 'dp', scatter_dimensi...]
    unnamed x212 -> x204, local copies, waits for them, and re-layouts: 44.7 us -> 36.7 us
  transfers between devices with their start and end apart: 59 -> 60, of which waited for: 27 -> 30; matrix products, arithmetic and copies ran while one was open for 27% -> 24% of each run, Pallas kernels for 0% -> 0%
where the time goes in v1:
time: 1520 us
  waiting for transfers between devices  884 us (58%)
  matrix products  236 us (16%)
  other arithmetic  151 us (10%)
  blocking collectives  95 us (6%)
  starting transfers between devices  93.3 us (6%)
  local copies, waits for them, and re-layouts  41.1 us (3%)
  between operations  16.2 us (1%)
    ppermute x52, waiting for transfers between devices, swapped(): lax.ppermute(x, axis, [(i, i ^ 1 << bit) for i in range(lax.axis_size(axi...  578 us
    psum x1, waiting for transfers between devices, on_device(): small_sums = lax.psum(partial, 'tensor')  116 us
    ppermute x52, starting transfers between devices, swapped(): lax.ppermute(x, axis, [(i, i ^ 1 << bit) for i in range(lax.axis_size(axi...  92.6 us
    psum x1, waiting for transfers between devices, on_device(): lax.psum((front_grads[1], front_grads[2], front_grads[3], front_grads[4],...  78.7 us
    reduce_scatter x1, waiting for transfers between devices, on_device(): lax.psum_scatter(grad_w_key.astype(jnp.bfloat16), 'dp', scatter_dimension...  72.3 us
    dot_general x3, matrix products, front_part(): jnp.einsum('tkj,jtd->ktd', mixing, history_float, precision=PRECISE)  63.2 us
    psum x1, blocking collectives, on_device(): small_sums = lax.psum(partial, 'tensor')  63 us
    dot_general x6, matrix products, across_cols(): lax.dot_general(left_side, right_side, (((1,), (1,)), ((), ())), preferre...  43.8 us
  transfers between devices with their start and end apart: 60, of which 30 were waited for; matrix products, arithmetic and copies ran while one was open for 24% of the time, Pallas kernels for 0%

profile of v1, /device:TPU:1, one launch (start us, length us, event | category | flops | bytes accessed | tf_op | source)
XLA Modules:
  0.0 1517.1 jit_solution(8852213992614347593)
XLA Ops:
  15.3 19.8 %fusion.22 = f32[4,128,2048]{2,0,1:T(4,128)S(1)} fusion(f32[128,4,17]{2,1,0:T(4,128)S(1)} %copy.62, bf16[17,128,2048]{2,1,0:T(8,128)(2,1)} %param.17), kind=kOutput, calls=%fused_computation.55 | convolution fusion | flops 213909504 | bytes 13142016 | tf_op jit(solution)/shard_map/jvp(tkj,jtd->ktd)/dot_general | solution.py:35
  50.3 16.2 %collective-permute-done.10 = bf16[128,2048]{1,0:T(8,128)(2,1)} collective-permute-done((bf16[128,2048]{1,0:T(8,128)(2,1)S(1)}, bf16[128,2048]{1,0:T(8,128)(2,1)}, u32[]{:S(2)}, u32[]{:S(2)}) %collective-permute-start.10) | collective-permute-done | bytes 524320 | tf_op jit(solution)/shard_map/ppermute | solution.py:15
  80.4 19.8 %collective-permute-done.6 = bf16[128,2048]{1,0:T(8,128)(2,1)S(1)} collective-permute-done((bf16[128,2048]{1,0:T(8,128)(2,1)S(1)}, bf16[128,2048]{1,0:T(8,128)(2,1)S(1)}, u32[]{:S(2)}, u32[]{:S(2)}) %collective-permute-start.6) | collective-permute-done | bytes 524320 | tf_op jit(solution)/shard_map/ppermute | solution.py:15
  102.0 5.0 convolution_convert_fusion.1
  109.8 13.2 collective-permute-done.3
  132.0 13.5 collective-permute-done.9
  150.5 17.4 %collective-permute-done.15 = bf16[1024,512]{0,1:T(8,128)(2,1)S(1)} collective-permute-done((bf16[1024,512]{0,1:T(8,128)(2,1)S(1)}, bf16[1024,512]{0,1:T(8,128)(2,1)S(1)}, u32[]{:S(2)}, u32[]{:S(2)}) %collective-permute-start.15) | collective-permute-done | bytes 1048608 | tf_op jit(solution)/shard_map/ppermute | solution.py:15
  167.9 8.6 fusion.112
  176.6 8.1 fusion.1
  184.7 28.3 %collective-permute-done.5 = bf16[1024,512]{0,1:T(8,128)(2,1)} collective-permute-done((bf16[1024,512]{0,1:T(8,128)(2,1)}, bf16[1024,512]{0,1:T(8,128)(2,1)}, u32[]{:S(2)}, u32[]{:S(2)}) %collective-permute-start.5) | collective-permute-done | bytes 1048608 | tf_op jit(solution)/shard_map/ppermute | solution.py:15
  213.0 8.3 fusion.30
  226.5 5.1 maximum_select_fusion.2
  232.8 16.3 %collective-permute-done.18 = bf16[256,2048]{1,0:T(8,128)(2,1)S(1)} collective-permute-done((bf16[256,2048]{1,0:T(8,128)(2,1)S(1)}, bf16[256,2048]{1,0:T(8,128)(2,1)S(1)}, u32[]{:S(2)}, u32[]{:S(2)}) %collective-permute-start.18) | collective-permute-done | bytes 1048608 | tf_op jit(solution)/shard_map/ppermute | solution.py:15
  253.4 80.9 %collective-permute-done.19 = bf16[128,2048]{1,0:T(8,128)(2,1)S(1)} collective-permute-done((bf16[128,2048]{1,0:T(8,128)(2,1)S(1)}, bf16[128,2048]{1,0:T(8,128)(2,1)S(1)}, u32[]{:S(2)}, u32[]{:S(2)}) %collective-permute-start.19) | collective-permute-done | bytes 524320 | tf_op jit(solution)/shard_map/ppermute | solution.py:15
  337.6 11.0 collective-permute-done.20
  351.1 3.7 maximum_select_fusion.3
  355.2 6.0 collective-permute-done.28
  365.2 5.8 collective-permute-done.21
  371.0 26.4 %multiply_convert_fusion.1 = (bf16[512,2048]{1,0:T(8,128)(2,1)}, f32[512,2048]{1,0:T(8,128)}, f32[512,2048]{1,0:T(8,128)}) fusion(bf16[2048,1024]{1,0:T(8,128)(2,1)} %copy-done.19, bf16[2048,1024]{1,0:T(8,128)(2,1)} %copy-done.76, pred[]{:T(512)S(6)} %eq.154, bf16[256,2048]{1,0:T(8,128)(2,1)} %copy-done.38, bf16[256,2048]{1,0:T(8,128)(2,1)} %collective-permute-done.21, ...), kind=kOutput, calls=%fused_computation.37 | convolution fusion | flops 4410310656 | bytes 20971522 | tf_op jit(solution)/shard_map/dot_general | solution.py:218
  397.5 52.7 %collective-permute-done.25 = bf16[1024,2048]{1,0:T(8,128)(2,1)} collective-permute-done((bf16[1024,2048]{1,0:T(8,128)(2,1)}, bf16[1024,2048]{1,0:T(8,128)(2,1)}, u32[]{:S(2)}, u32[]{:S(2)}) %collective-permute-start.25) | collective-permute-done | bytes 4194336 | tf_op jit(solution)/shard_map/ppermute | solution.py:15
  450.1 20.4 %add_convert_fusion.2 = bf16[512,2048]{1,0:T(8,128)(2,1)} fusion(f32[512,2048]{1,0:T(8,128)} %get-tuple-element.163, f32[512,2048]{1,0:T(8,128)} %get-tuple-element.178, bf16[1024,2048]{1,0:T(8,128)(2,1)} %maximum_select_fusion.3, bf16[1024,2048]{1,0:T(8,128)(2,1)} %collective-permute-done.25, pred[]{:T(512)S(6)} %eq.154, ...), kind=kOutput, calls=%fused_computation.36 | convolution fusion | flops 4356833280 | bytes 20971522 | tf_op jit(solution)/shard_map/dot_general | solution.py:55
  470.5 10.6 fusion.27
  481.3 10.2 fusion.26
  493.5 7.0 fusion.54
  500.5 34.4 %collective-permute-done.30 = bf16[256,2048]{1,0:T(8,128)(2,1)} collective-permute-done((bf16[256,2048]{1,0:T(8,128)(2,1)S(1)}, bf16[256,2048]{1,0:T(8,128)(2,1)}, u32[]{:S(2)}, u32[]{:S(2)}) %collective-permute-start.30) | collective-permute-done | bytes 1048608 | tf_op jit(solution)/shard_map/ppermute | solution.py:15
  543.0 4.5 collective-permute-done.31
  548.7 10.4 collective-permute-done.27
  565.7 4.7 collective-permute-done.32
  572.0 7.2 fusion.53
  579.2 5.8 copy-done.3
  589.0 4.3 convolution_convert_fusion
  598.0 14.3 multiply_reduce_fusion
  612.3 15.9 %multiply_convert_fusion = bf16[4,512,2048]{2,1,0:T(8,128)(2,1)} fusion(f32[4,512,2048]{2,1,0:T(8,128)} %get-tuple-element.180, f32[4,512,2048]{2,1,0:T(8,128)} %get-tuple-element.177, f32[4,512]{1,0:T(4,128)S(1)} %get-tuple-element.179, f32[4,512]{1,0:T(4,128)S(1)} %log_add_fusion), kind=kLoop, calls=%fused_computation.2 | loop fusion | flops 16777216 | bytes 41959424 | tf_op jit(solution)/shard_map/while/body/eval_jaxpr/convert_element_type | solution.py:256
  628.2 6.3 fusion.29
  634.6 4.9 multiply_bitcast_fusion
  650.4 121.4 %collective-permute-done.46 = bf16[256,2048]{1,0:T(8,128)(2,1)S(1)} collective-permute-done((bf16[256,2048]{1,0:T(8,128)(2,1)S(1)}, bf16[256,2048]{1,0:T(8,128)(2,1)S(1)}, u32[]{:S(2)}, u32[]{:S(2)}) %collective-permute-start.46) | collective-permute-done | bytes 1048608 | tf_op jit(solution)/shard_map/ppermute | solution.py:15
  772.7 21.6 %collective-permute-done.36 = bf16[1024,512]{0,1:T(8,128)(2,1)S(1)} collective-permute-done((bf16[1024,512]{0,1:T(8,128)(2,1)S(1)}, bf16[1024,512]{0,1:T(8,128)(2,1)S(1)}, u32[]{:S(2)}, u32[]{:S(2)}) %collective-permute-start.36) | collective-permute-done | bytes 1048608 | tf_op jit(solution)/shard_map/ppermute | solution.py:15
  794.3 12.9 collective-permute-start.47
  808.5 8.2 collective-permute-done.34
  816.8 12.9 collective-permute-start.37
  830.9 8.3 collective-permute-done.40
  839.2 6.7 collective-permute-start.35
  846.5 7.4 convert_add_fusion.1
  858.0 3.8 fusion.63
  878.4 5.4 fusion.59
  894.5 18.2 %collective-permute-done.42 = bf16[2048,256]{1,0:T(8,128)(2,1)} collective-permute-done((bf16[2048,256]{1,0:T(8,128)(2,1)S(1)}, bf16[2048,256]{1,0:T(8,128)(2,1)}, u32[]{:S(2)}, u32[]{:S(2)}) %collective-permute-start.42) | collective-permute-done | bytes 1048608 | tf_op jit(solution)/shard_map/ppermute | solution.py:15
  915.3 34.9 %collective-permute-done.38 = bf16[256,6144]{1,0:T(8,128)(2,1)} collective-permute-done((bf16[256,6144]{1,0:T(8,128)(2,1)}, bf16[256,6144]{1,0:T(8,128)(2,1)}, u32[]{:S(2)}, u32[]{:S(2)}) %collective-permute-start.38) | collective-permute-done | bytes 3145760 | tf_op jit(solution)/shard_map/ppermute | solution.py:15
  950.2 7.4 convert_add_fusion.2
  964.7 5.2 select_convert_fusion.4
  973.5 24.9 %collective-permute-done.39 = bf16[128,6144]{1,0:T(8,128)(2,1)} collective-permute-done((bf16[128,6144]{1,0:T(8,128)(2,1)}, bf16[128,6144]{1,0:T(8,128)(2,1)}, u32[]{:S(2)}, u32[]{:S(2)}) %collective-permute-start.39) | collective-permute-done | bytes 1572896 | tf_op jit(solution)/shard_map/ppermute | solution.py:15
  998.4 3.8 convert_add_fusion.3
  1008.2 17.9 %fusion.113 = (f32[4,17]{1,0:T(4,128)S(1)}, f32[128,4,17]{2,1,0:T(4,128)S(1)}) fusion(bf16[17,128,2048]{2,1,0:T(8,128)(2,1)S(1)} %bitcast.136, f32[128,2048,4]{1,0,2:T(8,128)S(1)} %add_bitcast_fusion), kind=kOutput, calls=%fused_computation.270 | convolution fusion | flops 213918144 | bytes 13142288 | tf_op jit(solution)/shard_map/transpose(jvp(tkj,jtd->ktd))/dot_general | solution.py:35
  1029.4 6.7 add_convert_fusion.1
  1036.2 8.7 convert_add_fusion
  1047.2 3.8 collective-permute-done.51
  1056.6 16.9 %reduce-scatter.11.cloned.1.call-done = bf16[256,128]{1,0:T(8,128)(2,1)} async-done(((bf16[2048,128]{1,0:T(8,128)(2,1)}), bf16[256,128]{1,0:T(8,128)(2,1)}) %reduce-scatter.11.cloned.1.call-update) | async-done | bytes 65552 | tf_op jit(solution)/shard_map/reduce_scatter | solution.py:330
  1075.0 72.3 %reduce-scatter.9.cloned.1.call-done = bf16[256,128]{1,0:T(8,128)(2,1)} async-done(((bf16[2048,128]{1,0:T(8,128)(2,1)}), bf16[256,128]{1,0:T(8,128)(2,1)}) %reduce-scatter.9.cloned.1.call-update) | async-done | bytes 65552 | tf_op jit(solution)/shard_map/reduce_scatter | solution.py:327
  1153.4 78.7 %all-reduce.10.cloned.1.call-done = f32[2048,68]{0,1:T(8,128)} async-done(((f32[2048,68]{0,1:T(8,128)}), f32[2048,68]{0,1:T(8,128)}) %all-reduce.10.cloned.1.call-update) | async-done | bytes 557072 | tf_op jit(solution)/shard_map/psum | solution.py:309
  1232.1 25.5 %fusion = bf16[17,128,2048]{2,0,1:T(8,128)(2,1)} fusion(f32[1,128,2048]{2,0,1:T(1,128)S(1)} %broadcast_in_dim.111, f32[128,4,17]{2,1,0:T(4,128)S(1)} %copy-done.27, f32[128,2048,4]{1,0,2:T(8,128)} %copy-done.18), kind=kOutput, calls=%fused_computation.1 | convolution fusion | flops 222822400 | bytes 14190592 | tf_op jit(solution)/shard_map/transpose(jvp(tkj,jtd->ktd))/dot_general | solution.py:35
  1257.7 13.6 copy.76
  1271.6 31.9 %all-reduce.6 = (f32[2048]{0:T(1024)S(1)}, f32[68,68]{1,0:T(8,128)S(1)}, f32[68]{0:T(128)S(1)}, f32[2048]{0:T(1024)S(1)}, f32[2048]{0:T(1024)S(1)}, /*index=5*/f32[2048]{0:T(1024)S(1)}, f32[2048]{0:T(1024)S(1)}) all-reduce(f32[2048]{0:T(1024)S(1)} %get-tuple-element.133, ...), channel_id=1, replica_groups=mesh['dp'=8,'tensor'=16] {'dp'}, use_global_device_ids=true, to_apply=%region_17.18 | all-reduce | flops 14932 | bytes 119456 | tf_op jit(solution)/shard_map/psum | solution.py:309
  1303.6 63.0 %all-reduce.5 = (f32[2048]{0:T(1024)}, f32[68,68]{1,0:T(8,128)}, f32[68]{0:T(128)}, f32[2048]{0:T(1024)}, f32[2048]{0:T(1024)}, /*index=5*/f32[2048]{0:T(1024)}, f32[2048]{0:T(1024)}) all-reduce(f32[2048]{0:T(1024)S(1)} %get-tuple-element.154, f32[68,68]{1,0:T(8,128)S(1)} %get-tuple-element.155, ...), channel_id=1, replica_groups=mesh['dp'=8,'tensor'=16] {'tensor'}, use_global_device_ids=true, to_apply=%region_18.19 | all-reduce | flops 14932 | bytes 119456 | tf_op jit(solution)/shard_map/psum | solution.py:322
  1368.4 21.8 %reduce-scatter.17.cloned.1.call-done = bf16[512,256]{1,0:T(8,128)(2,1)} async-done(((bf16[512,2048]{1,0:T(8,128)(2,1)}), bf16[512,256]{1,0:T(8,128)(2,1)}) %reduce-scatter.17.cloned.1.call-update) | async-done | bytes 262160 | tf_op jit(solution)/shard_map/reduce_scatter | solution.py:339
  1392.0 116.1 %all-reduce.12.cloned.1.call-done = f32[2048,68]{0,1:T(8,128)} async-done(((f32[2048,68]{0,1:T(8,128)}), f32[2048,68]{0,1:T(8,128)}) %all-reduce.12.cloned.1.call-update) | async-done | bytes 557072 | tf_op jit(solution)/shard_map/psum | solution.py:322
  (420 shorter events, 193.9 us)
Async XLA Ops:
  7.2 1046.4 %reduce-scatter.13.cloned.1.call-start = ((), (), s32[]{:S(2)}) async-start(), calls=%async_computation.11 | async-start | bytes 589824 | tf_op jit(solution)/shard_map/reduce_scatter | solution.py:333
  7.2 68.0 %collective-permute-start.8 = (bf16[2048,128]{1,0:T(8,128)(2,1)}, bf16[2048,128]{1,0:T(8,128)(2,1)}, u32[]{:S(2)}, u32[]{:S(2)}) collective-permute-start(bf16[2048,128]{1,0:T(8,128)(2,1)} %param.28), channel_id=1, source_target_pairs={{0,1},{1,0},{2,3},{3,2},{4,5},{5,4},{6,7},{7,6},{8,9},{9,8},{10,11... | collective-permute-start | bytes 1572872 | tf_op jit(solution)/shard_map/ppermute | solution.py:15
  8.7 37.5 %collective-permute-start.12 = (bf16[2048,128]{1,0:T(8,128)(2,1)}, bf16[2048,128]{1,0:T(8,128)(2,1)}, u32[]{:S(2)}, u32[]{:S(2)}) collective-permute-start(bf16[2048,128]{1,0:T(8,128)(2,1)} %param.29), channel_id=1, source_target_pairs={{0,1},{1,0},{2,3},{3,2},{4,5},{5,4},{6,7},{7,6},{8,9},{9,8},{10,11... | collective-permute-start | bytes 1572872 | tf_op jit(solution)/shard_map/ppermute | solution.py:15
  8.8 61.6 %collective-permute-start.2 = (bf16[2048,128]{1,0:T(8,128)(2,1)}, bf16[2048,128]{1,0:T(8,128)(2,1)}, u32[]{:S(2)}, u32[]{:S(2)}) collective-permute-start(bf16[2048,128]{1,0:T(8,128)(2,1)} %param.30), channel_id=1, source_target_pairs={{0,1},{1,0},{2,3},{3,2},{4,5},{5,4},{6,7},{7,6},{8,9},{9,8},{10,11... | collective-permute-start | bytes 1572872 | tf_op jit(solution)/shard_map/ppermute | solution.py:15
  39.7 37.9 %collective-permute-start = (bf16[128,2048]{1,0:T(8,128)(2,1)S(1)}, bf16[128,2048]{1,0:T(8,128)(2,1)}, u32[]{:S(2)}, u32[]{:S(2)}) collective-permute-start(bf16[128,2048]{1,0:T(8,128)(2,1)S(1)} %multiply_convert_fusion.5), channel_id=1, source_target_pairs={{0,4},{1,5},{2,6},{3,7},{4,0},{5,1},{6,2},{7,3},{8,12},{9,13},{10,... | collective-permute-start | bytes 1572872 | tf_op jit(solution)/shard_map/ppermute | solution.py:15
  44.0 22.5 %collective-permute-start.10 = (bf16[128,2048]{1,0:T(8,128)(2,1)S(1)}, bf16[128,2048]{1,0:T(8,128)(2,1)}, u32[]{:S(2)}, u32[]{:S(2)}) collective-permute-start(bf16[128,2048]{1,0:T(8,128)(2,1)S(1)} %multiply_convert_fusion.3), channel_id=1, source_target_pairs={{0,4},{1,5},{2,6},{3,7},{4,0},{5,1},{6,2},{7,3},{8,12},{9,13},{10,... | collective-permute-start | bytes 1572872 | tf_op jit(solution)/shard_map/ppermute | solution.py:15
  49.0 52.7 %collective-permute-start.13 = (bf16[2048,256]{1,0:T(8,128)(2,1)}, bf16[2048,256]{1,0:T(8,128)(2,1)}, u32[]{:S(2)}, u32[]{:S(2)}) collective-permute-start(bf16[2048,256]{1,0:T(8,128)(2,1)} %maximum_select_fusion.29), channel_id=1, source_target_pairs={{0,2},{1,3},{2,0},{3,1},{4,6},{5,7},{6,4},{7,5},{8,10},{9,11},{10,... | collective-permute-start | bytes 3145736 | tf_op jit(solution)/shard_map/ppermute | solution.py:15
  69.1 32.9 %collective-permute-start.11 = (bf16[256,2048]{1,0:T(8,128)(2,1)}, bf16[256,2048]{1,0:T(8,128)(2,1)}, u32[]{:S(2)}, u32[]{:S(2)}) collective-permute-start(bf16[256,2048]{1,0:T(8,128)(2,1)} %maximum_select_fusion.28), channel_id=1, source_target_pairs={{0,8},{1,9},{2,10},{3,11},{4,12},{5,13},{6,14},{7,15},{8,0},{9,1},... | collective-permute-start | bytes 3145736 | tf_op jit(solution)/shard_map/ppermute | solution.py:15
  70.4 29.7 %collective-permute-start.6 = (bf16[128,2048]{1,0:T(8,128)(2,1)S(1)}, bf16[128,2048]{1,0:T(8,128)(2,1)S(1)}, u32[]{:S(2)}, u32[]{:S(2)}) collective-permute-start(bf16[128,2048]{1,0:T(8,128)(2,1)S(1)} %multiply_convert_fusion.4), channel_id=1, source_target_pairs={{0,4},{1,5},{2,6},{3,7},{4,0},{5,1},{6,2},{7,3},{8,12},{9,13},{10,... | collective-permute-start | bytes 1572872 | tf_op jit(solution)/shard_map/ppermute | solution.py:15
  75.3 47.7 %collective-permute-start.3 = (bf16[2048,256]{1,0:T(8,128)(2,1)S(1)}, bf16[2048,256]{1,0:T(8,128)(2,1)S(1)}, u32[]{:S(2)}, u32[]{:S(2)}) collective-permute-start(bf16[2048,256]{1,0:T(8,128)(2,1)S(1)} %maximum_select_fusion.23), channel_id=1, source_target_pairs={{0,2},{1,3},{2,0},{3,1},{4,6},{5,7},{6,4},{7,5},{8,10},{9,11},{10,... | collective-permute-start | bytes 3145736 | tf_op jit(solution)/shard_map/ppermute | solution.py:15
  77.6 67.8 %collective-permute-start.9 = (bf16[2048,256]{1,0:T(8,128)(2,1)S(1)}, bf16[2048,256]{1,0:T(8,128)(2,1)S(1)}, u32[]{:S(2)}, u32[]{:S(2)}) collective-permute-start(bf16[2048,256]{1,0:T(8,128)(2,1)S(1)} %maximum_select_fusion.27), channel_id=1, source_target_pairs={{0,2},{1,3},{2,0},{3,1},{4,6},{5,7},{6,4},{7,5},{8,10},{9,11},{10,... | collective-permute-start | bytes 3145736 | tf_op jit(solution)/shard_map/ppermute | solution.py:15
  100.1 24.2 %collective-permute-start.1 = (bf16[256,2048]{1,0:T(8,128)(2,1)S(1)}, bf16[256,2048]{1,0:T(8,128)(2,1)S(1)}, u32[]{:S(2)}, u32[]{:S(2)}) collective-permute-start(bf16[256,2048]{1,0:T(8,128)(2,1)S(1)} %maximum_select_fusion.22), channel_id=1, source_target_pairs={{0,8},{1,9},{2,10},{3,11},{4,12},{5,13},{6,14},{7,15},{8,0},{9,1},... | collective-permute-start | bytes 3145736 | tf_op jit(solution)/shard_map/ppermute | solution.py:15
  101.7 45.0 %collective-permute-start.7 = (bf16[256,2048]{1,0:T(8,128)(2,1)S(1)}, bf16[256,2048]{1,0:T(8,128)(2,1)S(1)}, u32[]{:S(2)}, u32[]{:S(2)}) collective-permute-start(bf16[256,2048]{1,0:T(8,128)(2,1)S(1)} %maximum_select_fusion.26), channel_id=1, source_target_pairs={{0,8},{1,9},{2,10},{3,11},{4,12},{5,13},{6,14},{7,15},{8,0},{9,1},... | collective-permute-start | bytes 3145736 | tf_op jit(solution)/shard_map/ppermute | solution.py:15
  107.0 21.9 %collective-permute-start.14 = (bf16[512,512]{0,1:T(8,128)(2,1)S(1)}, bf16[512,512]{0,1:T(8,128)(2,1)S(1)}, u32[]{:S(2)}, u32[]{:S(2)}) collective-permute-start(bf16[512,512]{0,1:T(8,128)(2,1)S(1)} %convolution_convert_fusion.1), channel_id=1, source_target_pairs={{0,1},{1,0},{2,3},{3,2},{4,5},{5,4},{6,7},{7,6},{8,9},{9,8},{10,11... | collective-permute-start | bytes 1572872 | tf_op jit(solution)/shard_map/ppermute | solution.py:15
  123.0 6.3 collective-permute-start.16
  124.4 102.2 %collective-permute-start.22 = (bf16[2048,512]{1,0:T(8,128)(2,1)}, bf16[2048,512]{1,0:T(8,128)(2,1)}, u32[]{:S(2)}, u32[]{:S(2)}) collective-permute-start(bf16[2048,512]{1,0:T(8,128)(2,1)} %param.32), channel_id=1, source_target_pairs={{0,1},{1,0},{2,3},{3,2},{4,5},{5,4},{6,7},{7,6},{8,9},{9,8},{10,11... | collective-permute-start | bytes 6291464 | tf_op jit(solution)/shard_map/ppermute | solution.py:15
  128.9 19.2 %collective-permute-start.4 = (bf16[512,512]{0,1:T(8,128)(2,1)S(1)}, bf16[512,512]{0,1:T(8,128)(2,1)S(1)}, u32[]{:S(2)}, u32[]{:S(2)}) collective-permute-start(bf16[512,512]{0,1:T(8,128)(2,1)S(1)} %convolution_convert_fusion.3), channel_id=1, source_target_pairs={{0,1},{1,0},{2,3},{3,2},{4,5},{5,4},{6,7},{7,6},{8,9},{9,8},{10,11... | collective-permute-start | bytes 1572872 | tf_op jit(solution)/shard_map/ppermute | solution.py:15
  129.3 38.6 %collective-permute-start.15 = (bf16[1024,512]{0,1:T(8,128)(2,1)S(1)}, bf16[1024,512]{0,1:T(8,128)(2,1)S(1)}, u32[]{:S(2)}, u32[]{:S(2)}) collective-permute-start(bf16[1024,512]{0,1:T(8,128)(2,1)S(1)} %maximum_select_fusion.30), channel_id=1, source_target_pairs={{0,2},{1,3},{2,0},{3,1},{4,6},{5,7},{6,4},{7,5},{8,10},{9,11},{10,... | collective-permute-start | bytes 3145736 | tf_op jit(solution)/shard_map/ppermute | solution.py:15
  145.5 75.9 %collective-permute-start.17 = (bf16[256,2048]{1,0:T(8,128)(2,1)}, bf16[256,2048]{1,0:T(8,128)(2,1)}, u32[]{:S(2)}, u32[]{:S(2)}) collective-permute-start(bf16[256,2048]{1,0:T(8,128)(2,1)} %maximum_select_fusion.32), channel_id=1, source_target_pairs={{0,2},{1,3},{2,0},{3,1},{4,6},{5,7},{6,4},{7,5},{8,10},{9,11},{10,... | collective-permute-start | bytes 3145736 | tf_op jit(solution)/shard_map/ppermute | solution.py:15
  149.3 63.7 %collective-permute-start.5 = (bf16[1024,512]{0,1:T(8,128)(2,1)}, bf16[1024,512]{0,1:T(8,128)(2,1)}, u32[]{:S(2)}, u32[]{:S(2)}) collective-permute-start(bf16[1024,512]{0,1:T(8,128)(2,1)} %maximum_select_fusion.24), channel_id=1, source_target_pairs={{0,2},{1,3},{2,0},{3,1},{4,6},{5,7},{6,4},{7,5},{8,10},{9,11},{10,... | collective-permute-start | bytes 3145736 | tf_op jit(solution)/shard_map/ppermute | solution.py:15
  225.2 23.9 %collective-permute-start.18 = (bf16[256,2048]{1,0:T(8,128)(2,1)S(1)}, bf16[256,2048]{1,0:T(8,128)(2,1)S(1)}, u32[]{:S(2)}, u32[]{:S(2)}) collective-permute-start(bf16[256,2048]{1,0:T(8,128)(2,1)S(1)} %select_convert_fusion.14), channel_id=1, source_target_pairs={{0,8},{1,9},{2,10},{3,11},{4,12},{5,13},{6,14},{7,15},{8,0},{9,1},... | collective-permute-start | bytes 3145736 | tf_op jit(solution)/shard_map/ppermute | solution.py:15
  231.7 131.5 %collective-permute-start.23 = (bf16[2048,1024]{1,0:T(8,128)(2,1)S(1)}, bf16[2048,1024]{1,0:T(8,128)(2,1)S(1)}, u32[]{:S(2)}, u32[]{:S(2)}) collective-permute-start(bf16[2048,1024]{1,0:T(8,128)(2,1)S(1)} %maximum_select_fusion.2), channel_id=1, source_target_pairs={{0,2},{1,3},{2,0},{3,1},{4,6},{5,7},{6,4},{7,5},{8,10},{9,11},{10,... | collective-permute-start | bytes 12582920 | tf_op jit(solution)/shard_map/ppermute | solution.py:15
  249.6 85.6 %copy-start.47 = (f32[2048]{0:T(1024)S(1)}, f32[2048]{0:T(1024)}, u32[]{:S(2)}) copy-start(f32[2048]{0:T(1024)} %param.27) | copy-start | bytes 24580
  249.7 84.6 %collective-permute-start.19 = (bf16[128,2048]{1,0:T(8,128)(2,1)S(1)}, bf16[128,2048]{1,0:T(8,128)(2,1)S(1)}, u32[]{:S(2)}, u32[]{:S(2)}) collective-permute-start(bf16[128,2048]{1,0:T(8,128)(2,1)S(1)} %select_convert_fusion.23), channel_id=1, source_target_pairs={{0,4},{1,5},{2,6},{3,7},{4,0},{5,1},{6,2},{7,3},{8,12},{9,13},{10,... | collective-permute-start | bytes 1572872 | tf_op jit(solution)/shard_map/ppermute | solution.py:15
  251.4 99.7 %collective-permute-start.24 = (bf16[512,2048]{1,0:T(8,128)(2,1)S(1)}, bf16[512,2048]{1,0:T(8,128)(2,1)S(1)}, u32[]{:S(2)}, u32[]{:S(2)}) collective-permute-start(bf16[512,2048]{1,0:T(8,128)(2,1)S(1)} %copy-done.25), channel_id=1, source_target_pairs={{0,1},{1,0},{2,3},{3,2},{4,5},{5,4},{6,7},{7,6},{8,9},{9,8},{10,11... | collective-permute-start | bytes 6291464 | tf_op jit(solution)/shard_map/ppermute | solution.py:15
  335.4 13.2 collective-permute-start.20
  348.9 22.1 %collective-permute-start.21 = (bf16[256,2048]{1,0:T(8,128)(2,1)S(1)}, bf16[256,2048]{1,0:T(8,128)(2,1)}, u32[]{:S(2)}, u32[]{:S(2)}) collective-permute-start(bf16[256,2048]{1,0:T(8,128)(2,1)S(1)} %maximum_select_fusion.33), channel_id=1, source_target_pairs={{0,8},{1,9},{2,10},{3,11},{4,12},{5,13},{6,14},{7,15},{8,0},{9,1},... | collective-permute-start | bytes 3145736 | tf_op jit(solution)/shard_map/ppermute | solution.py:15
  349.2 12.0 collective-permute-start.28
  354.8 95.3 %collective-permute-start.25 = (bf16[1024,2048]{1,0:T(8,128)(2,1)}, bf16[1024,2048]{1,0:T(8,128)(2,1)}, u32[]{:S(2)}, u32[]{:S(2)}) collective-permute-start(bf16[1024,2048]{1,0:T(8,128)(2,1)} %maximum_select_fusion.3), channel_id=1, source_target_pairs={{0,2},{1,3},{2,0},{3,1},{4,6},{5,7},{6,4},{7,5},{8,10},{9,11},{10,... | collective-permute-start | bytes 12582920 | tf_op jit(solution)/shard_map/ppermute | solution.py:15
  361.4 88.7 %copy-start.37 = (bf16[256,2048]{1,0:T(8,128)(2,1)}, bf16[256,2048]{1,0:T(8,128)(2,1)S(1)}, u32[]{:S(2)}) copy-start(bf16[256,2048]{1,0:T(8,128)(2,1)S(1)} %maximum_select_fusion.34) | copy-start | bytes 3145732
  361.4 36.0 %collective-permute-start.29 = (bf16[256,2048]{1,0:T(8,128)(2,1)S(1)}, bf16[256,2048]{1,0:T(8,128)(2,1)}, u32[]{:S(2)}, u32[]{:S(2)}) collective-permute-start(bf16[256,2048]{1,0:T(8,128)(2,1)S(1)} %maximum_select_fusion.34), channel_id=1, source_target_pairs={{0,8},{1,9},{2,10},{3,11},{4,12},{5,13},{6,14},{7,15},{8,0},{9,1},... | collective-permute-start | bytes 3145736 | tf_op jit(solution)/shard_map/ppermute | solution.py:15
  491.7 47.9 %collective-permute-start.26 = (bf16[256,2048]{1,0:T(8,128)(2,1)S(1)}, bf16[256,2048]{1,0:T(8,128)(2,1)}, u32[]{:S(2)}, u32[]{:S(2)}) collective-permute-start(bf16[256,2048]{1,0:T(8,128)(2,1)S(1)} %select_convert_fusion.13), channel_id=1, source_target_pairs={{0,8},{1,9},{2,10},{3,11},{4,12},{5,13},{6,14},{7,15},{8,0},{9,1},... | collective-permute-start | bytes 3145736 | tf_op jit(solution)/shard_map/ppermute | solution.py:15
  493.0 41.8 %collective-permute-start.30 = (bf16[256,2048]{1,0:T(8,128)(2,1)S(1)}, bf16[256,2048]{1,0:T(8,128)(2,1)}, u32[]{:S(2)}, u32[]{:S(2)}) collective-permute-start(bf16[256,2048]{1,0:T(8,128)(2,1)S(1)} %select_convert_fusion.12), channel_id=1, source_target_pairs={{0,8},{1,9},{2,10},{3,11},{4,12},{5,13},{6,14},{7,15},{8,0},{9,1},... | collective-permute-start | bytes 3145736 | tf_op jit(solution)/shard_map/ppermute | solution.py:15
  538.0 9.6 collective-permute-start.31
  541.5 17.5 %collective-permute-start.27 = (bf16[128,2048]{1,0:T(8,128)(2,1)S(1)}, bf16[128,2048]{1,0:T(8,128)(2,1)S(1)}, u32[]{:S(2)}, u32[]{:S(2)}) collective-permute-start(bf16[128,2048]{1,0:T(8,128)(2,1)S(1)} %select_convert_fusion.22), channel_id=1, source_target_pairs={{0,4},{1,5},{2,6},{3,7},{4,0},{5,1},{6,2},{7,3},{8,12},{9,13},{10,... | collective-permute-start | bytes 1572872 | tf_op jit(solution)/shard_map/ppermute | solution.py:15
  560.9 9.5 collective-permute-start.32
  564.8 281.5 %collective-permute-start.48 = (bf16[2048,1024]{1,0:T(8,128)(2,1)}, bf16[2048,1024]{1,0:T(8,128)(2,1)}, u32[]{:S(2)}, u32[]{:S(2)}) collective-permute-start(bf16[2048,1024]{1,0:T(8,128)(2,1)} %select_convert_fusion.1), channel_id=1, source_target_pairs={{0,2},{1,3},{2,0},{3,1},{4,6},{5,7},{6,4},{7,5},{8,10},{9,11},{10,... | collective-permute-start | bytes 12582920 | tf_op jit(solution)/shard_map/ppermute | solution.py:15
  570.8 18.3 %collective-permute-start.33 = (bf16[256,2048]{1,0:T(8,128)(2,1)S(1)}, bf16[256,2048]{1,0:T(8,128)(2,1)S(1)}, u32[]{:S(2)}, u32[]{:S(2)}) collective-permute-start(bf16[256,2048]{1,0:T(8,128)(2,1)S(1)} %maximum_select_fusion.35), channel_id=1, source_target_pairs={{0,8},{1,9},{2,10},{3,11},{4,12},{5,13},{6,14},{7,15},{8,0},{9,1},... | collective-permute-start | bytes 3145736 | tf_op jit(solution)/shard_map/ppermute | solution.py:15
  587.6 448.6 %collective-permute-start.50 = (bf16[1024,2048]{1,0:T(8,128)(2,1)}, bf16[1024,2048]{1,0:T(8,128)(2,1)}, u32[]{:S(2)}, u32[]{:S(2)}) collective-permute-start(bf16[1024,2048]{1,0:T(8,128)(2,1)} %select_convert_fusion), channel_id=1, source_target_pairs={{0,2},{1,3},{2,0},{3,1},{4,6},{5,7},{6,4},{7,5},{8,10},{9,11},{10,... | collective-permute-start | bytes 12582920 | tf_op jit(solution)/shard_map/ppermute | solution.py:15
  641.2 130.6 %collective-permute-start.46 = (bf16[256,2048]{1,0:T(8,128)(2,1)S(1)}, bf16[256,2048]{1,0:T(8,128)(2,1)S(1)}, u32[]{:S(2)}, u32[]{:S(2)}) collective-permute-start(bf16[256,2048]{1,0:T(8,128)(2,1)S(1)} %select_convert_fusion.6), channel_id=1, source_target_pairs={{0,2},{1,3},{2,0},{3,1},{4,6},{5,7},{6,4},{7,5},{8,10},{9,11},{10,... | collective-permute-start | bytes 3145736 | tf_op jit(solution)/shard_map/ppermute | solution.py:15
  642.6 151.7 %collective-permute-start.36 = (bf16[1024,512]{0,1:T(8,128)(2,1)S(1)}, bf16[1024,512]{0,1:T(8,128)(2,1)S(1)}, u32[]{:S(2)}, u32[]{:S(2)}) collective-permute-start(bf16[1024,512]{0,1:T(8,128)(2,1)S(1)} %bitcast.146), channel_id=1, source_target_pairs={{0,2},{1,3},{2,0},{3,1},{4,6},{5,7},{6,4},{7,5},{8,10},{9,11},{10,... | collective-permute-start | bytes 3145736 | tf_op jit(solution)/shard_map/ppermute | solution.py:15
  643.2 173.5 %collective-permute-start.34 = (bf16[1024,512]{0,1:T(8,128)(2,1)S(1)}, bf16[1024,512]{0,1:T(8,128)(2,1)S(1)}, u32[]{:S(2)}, u32[]{:S(2)}) collective-permute-start(bf16[1024,512]{0,1:T(8,128)(2,1)S(1)} %bitcast.145), channel_id=1, source_target_pairs={{0,2},{1,3},{2,0},{3,1},{4,6},{5,7},{6,4},{7,5},{8,10},{9,11},{10,... | collective-permute-start | bytes 3145736 | tf_op jit(solution)/shard_map/ppermute | solution.py:15
  771.8 67.4 %collective-permute-start.40 = (bf16[2048,256]{1,0:T(8,128)(2,1)S(1)}, bf16[2048,256]{1,0:T(8,128)(2,1)S(1)}, u32[]{:S(2)}, u32[]{:S(2)}) collective-permute-start(bf16[2048,256]{1,0:T(8,128)(2,1)S(1)} %select_convert_fusion.9), channel_id=1, source_target_pairs={{0,2},{1,3},{2,0},{3,1},{4,6},{5,7},{6,4},{7,5},{8,10},{9,11},{10,... | collective-permute-start | bytes 3145736 | tf_op jit(solution)/shard_map/ppermute | solution.py:15
  794.3 59.6 %collective-permute-start.47 = (bf16[128,2048]{1,0:T(8,128)(2,1)S(1)}, bf16[128,2048]{1,0:T(8,128)(2,1)}, u32[]{:S(2)}, u32[]{:S(2)}) collective-permute-start(bf16[128,2048]{1,0:T(8,128)(2,1)S(1)} %select_convert_fusion.15), channel_id=1, source_target_pairs={{0,1},{1,0},{2,3},{3,2},{4,5},{5,4},{6,7},{7,6},{8,9},{9,8},{10,11... | collective-permute-start | bytes 1572872 | tf_op jit(solution)/shard_map/ppermute | solution.py:15
  816.8 39.2 %collective-permute-start.37 = (bf16[512,512]{0,1:T(8,128)(2,1)}, bf16[512,512]{0,1:T(8,128)(2,1)}, u32[]{:S(2)}, u32[]{:S(2)}) collective-permute-start(bf16[512,512]{0,1:T(8,128)(2,1)} %select_convert_fusion.19), channel_id=1, source_target_pairs={{0,1},{1,0},{2,3},{3,2},{4,5},{5,4},{6,7},{7,6},{8,9},{9,8},{10,11... | collective-permute-start | bytes 1572872 | tf_op jit(solution)/shard_map/ppermute | solution.py:15
  839.2 28.1 %collective-permute-start.35 = (bf16[512,512]{0,1:T(8,128)(2,1)}, bf16[512,512]{0,1:T(8,128)(2,1)}, u32[]{:S(2)}, u32[]{:S(2)}) collective-permute-start(bf16[512,512]{0,1:T(8,128)(2,1)} %select_convert_fusion.20), channel_id=1, source_target_pairs={{0,1},{1,0},{2,3},{3,2},{4,5},{5,4},{6,7},{7,6},{8,9},{9,8},{10,11... | collective-permute-start | bytes 1572872 | tf_op jit(solution)/shard_map/ppermute | solution.py:15
  846.4 40.4 %collective-permute-start.41 = (bf16[2048,128]{1,0:T(8,128)(2,1)S(1)}, bf16[2048,128]{1,0:T(8,128)(2,1)}, u32[]{:S(2)}, u32[]{:S(2)}) collective-permute-start(bf16[2048,128]{1,0:T(8,128)(2,1)S(1)} %select_convert_fusion.18), channel_id=1, source_target_pairs={{0,1},{1,0},{2,3},{3,2},{4,5},{5,4},{6,7},{7,6},{8,9},{9,8},{10,11... | collective-permute-start | bytes 1572872 | tf_op jit(solution)/shard_map/ppermute | solution.py:15
  855.9 199.2 %reduce-scatter.7.cloned.1.call-start = ((), (), s32[]{:S(2)}) async-start(), calls=%async_computation.8 | async-start | bytes 589824 | tf_op jit(solution)/shard_map/reduce_scatter | solution.py:324
  865.0 25.3 %collective-permute-start.44 = (bf16[2048,256]{1,0:T(8,128)(2,1)}, bf16[2048,256]{1,0:T(8,128)(2,1)}, u32[]{:S(2)}, u32[]{:S(2)}) collective-permute-start(bf16[2048,256]{1,0:T(8,128)(2,1)} %select_convert_fusion.7), channel_id=1, source_target_pairs={{0,2},{1,3},{2,0},{3,1},{4,6},{5,7},{6,4},{7,5},{8,10},{9,11},{10,... | collective-permute-start | bytes 3145736 | tf_op jit(solution)/shard_map/ppermute | solution.py:15
  877.2 73.0 %collective-permute-start.38 = (bf16[256,6144]{1,0:T(8,128)(2,1)}, bf16[256,6144]{1,0:T(8,128)(2,1)}, u32[]{:S(2)}, u32[]{:S(2)}) collective-permute-start(bf16[256,6144]{1,0:T(8,128)(2,1)} %select_convert_fusion.2), channel_id=1, source_target_pairs={{0,8},{1,9},{2,10},{3,11},{4,12},{5,13},{6,14},{7,15},{8,0},{9,1},... | collective-permute-start | bytes 9437192 | tf_op jit(solution)/shard_map/ppermute | solution.py:15
  885.9 26.9 %collective-permute-start.42 = (bf16[2048,256]{1,0:T(8,128)(2,1)S(1)}, bf16[2048,256]{1,0:T(8,128)(2,1)}, u32[]{:S(2)}, u32[]{:S(2)}) collective-permute-start(bf16[2048,256]{1,0:T(8,128)(2,1)S(1)} %select_convert_fusion.8), channel_id=1, source_target_pairs={{0,2},{1,3},{2,0},{3,1},{4,6},{5,7},{6,4},{7,5},{8,10},{9,11},{10,... | collective-permute-start | bytes 3145736 | tf_op jit(solution)/shard_map/ppermute | solution.py:15
  888.9 184.6 %reduce-scatter.11.cloned.1.call-start = ((), (), s32[]{:S(2)}) async-start(), calls=%async_computation.10 | async-start | bytes 589824 | tf_op jit(solution)/shard_map/reduce_scatter | solution.py:330
  893.3 70.4 %collective-permute-start.45 = (bf16[2048,128]{1,0:T(8,128)(2,1)S(1)}, bf16[2048,128]{1,0:T(8,128)(2,1)S(1)}, u32[]{:S(2)}, u32[]{:S(2)}) collective-permute-start(bf16[2048,128]{1,0:T(8,128)(2,1)S(1)} %select_convert_fusion.16), channel_id=1, source_target_pairs={{0,1},{1,0},{2,3},{3,2},{4,5},{5,4},{6,7},{7,6},{8,9},{9,8},{10,11... | collective-permute-start | bytes 1572872 | tf_op jit(solution)/shard_map/ppermute | solution.py:15
  914.5 56.4 %collective-permute-start.43 = (bf16[2048,128]{1,0:T(8,128)(2,1)S(1)}, bf16[2048,128]{1,0:T(8,128)(2,1)}, u32[]{:S(2)}, u32[]{:S(2)}) collective-permute-start(bf16[2048,128]{1,0:T(8,128)(2,1)S(1)} %select_convert_fusion.17), channel_id=1, source_target_pairs={{0,1},{1,0},{2,3},{3,2},{4,5},{5,4},{6,7},{7,6},{8,9},{9,8},{10,11... | collective-permute-start | bytes 1572872 | tf_op jit(solution)/shard_map/ppermute | solution.py:15
  961.6 36.8 %collective-permute-start.39 = (bf16[128,6144]{1,0:T(8,128)(2,1)}, bf16[128,6144]{1,0:T(8,128)(2,1)}, u32[]{:S(2)}, u32[]{:S(2)}) collective-permute-start(bf16[128,6144]{1,0:T(8,128)(2,1)} %select_convert_fusion.5), channel_id=1, source_target_pairs={{0,4},{1,5},{2,6},{3,7},{4,0},{5,1},{6,2},{7,3},{8,12},{9,13},{10,... | collective-permute-start | bytes 4718600 | tf_op jit(solution)/shard_map/ppermute | solution.py:15
  964.7 182.7 %reduce-scatter.9.cloned.1.call-start = ((), (), s32[]{:S(2)}) async-start(), calls=%async_computation.9 | async-start | bytes 589824 | tf_op jit(solution)/shard_map/reduce_scatter | solution.py:327
  969.9 59.5 %collective-permute-start.49 = (bf16[2048,512]{1,0:T(8,128)(2,1)}, bf16[2048,512]{1,0:T(8,128)(2,1)}, u32[]{:S(2)}, u32[]{:S(2)}) collective-permute-start(bf16[2048,512]{1,0:T(8,128)(2,1)} %select_convert_fusion.4), channel_id=1, source_target_pairs={{0,1},{1,0},{2,3},{3,2},{4,5},{5,4},{6,7},{7,6},{8,9},{9,8},{10,11... | collective-permute-start | bytes 6291464 | tf_op jit(solution)/shard_map/ppermute | solution.py:15
  973.0 259.1 %all-reduce.10.cloned.1.call-start = ((), (), s32[]{:S(2)}) async-start(), calls=%async_computation.6 | async-start | bytes 1179648 | tf_op jit(solution)/shard_map/psum | solution.py:309
  1029.4 337.2 %reduce-scatter.15.cloned.1.call-start = ((), (), s32[]{:S(2)}) async-start(), calls=%async_computation.12 | async-start | bytes 2359296 | tf_op jit(solution)/shard_map/reduce_scatter | solution.py:336
  1036.1 354.1 %reduce-scatter.17.cloned.1.call-start = ((), (), s32[]{:S(2)}) async-start(), calls=%async_computation.13 | async-start | bytes 2359296 | tf_op jit(solution)/shard_map/reduce_scatter | solution.py:339
  1045.3 5.7 collective-permute-start.51
  1053.5 97.8 %copy-start.73 = (f32[128]{0:T(128)S(1)}, f32[128]{0:T(128)}, u32[]{:S(2)}) copy-start(f32[128]{0:T(128)} %copy-done.72) | copy-start | bytes 1540
  1053.5 454.5 %all-reduce.12.cloned.1.call-start = ((), (), s32[]{:S(2)}) async-start(), calls=%async_computation.7 | async-start | bytes 1179648 | tf_op jit(solution)/shard_map/psum | solution.py:322
  1075.0 157.1 %copy-start.27 = (f32[128,4,17]{2,1,0:T(4,128)S(1)}, f32[128,4,17]{2,1,0:T(4,128)}, u32[]{:S(2)}) copy-start(f32[128,4,17]{2,1,0:T(4,128)} %copy-done.26) | copy-start | bytes 104452
  (97 other events, 1412.2 us)
Sparse Core Ops, SparseCore 0:
  856.0 71.1 reduce-scatter.12
  931.8 69.1 reduce-scatter.6
  1004.5 68.9 reduce-scatter.10
  1077.9 69.4 reduce-scatter.8
  1150.3 81.7 all-reduce.9
  1235.6 76.8 reduce-scatter.14
  1316.3 73.8 reduce-scatter.16
  1392.7 115.3 all-reduce.11
